TPU v7x, 32 devices: a whole 2x2x4 slice. The times are simulated.
32 devices in a mesh: groups: 2 (over x), curve: 16 (over z, y, core).
Axes of the slice: x: 2, y: 2, z: 4, core: 2. Of those that a mesh axis runs over, the one named last changes fastest.
Arguments:
- fine_latent: bfloat16 [65536, 128], P(('groups', 'curve')), parts along dimension 0, may hold values from -6 to 6
- coarse_latent: bfloat16 [32768, 128], P(('groups', 'curve')), parts along dimension 0, may hold values from -6 to 6
- grad_coarse: bfloat16 [32768, 128], P(('groups', 'curve')), parts along dimension 0, may hold values from -6 to 6
- restrict_weights: bfloat16 [2, 32768], P(None, ('groups', 'curve')), parts along dimension 1, may hold values from 0.25 to 1
- send_rows: int32 [65536], P(('groups', 'curve')), parts along dimension 0, may hold values from 0 to 1024, as said below
- pair_slots: int32 [32768], P(('groups', 'curve')), parts along dimension 0, may hold values from 0 to 2047, as said below
- edge_receivers: int32 [196608], P(('groups', 'curve')), parts along dimension 0, may hold values from 0 to 2047
- edge_offsets: int32 [196608], P(('groups', 'curve')), parts along dimension 0, may hold values from -256 to 256
- edge_weight: bfloat16 [256, 128], replicated, may hold values from -0.375 to 0.375
- node_weight_in: bfloat16 [128, 128], replicated, may hold values from -0.5 to 0.5
- node_weight_out: bfloat16 [128, 128], replicated, may hold values from -0.5 to 0.5
- node_gain: float32 [128], replicated, may hold values from 0.5 to 2
Outputs:
- grad_fine: bfloat16 [65536, 128], P(('groups', 'curve')), parts along dimension 0
- grad_edge: float32 [512, 128], P('groups'), parts along dimension 0
- grad_node_in: float32 [256, 128], P('groups'), parts along dimension 0
- grad_node_out: float32 [256, 128], P('groups'), parts along dimension 0
- grad_gain: float32 [256], P('groups'), parts along dimension 0
There are 2 independent parts, one for each index of `groups`. A program takes and returns all parts, laid end to end along the dimension named above; an argument that names none is the same for every part. Nothing has to cross between parts.
Inputs may be any that keep to these rules, and one draw needn't show every extreme that they name: `send_rows`: in coarse shard d's block, entry s * 128 + t is the local coarse row sent in slot t toward fine shard s, and 1024 marks an empty slot. Every local coarse row is sent once; used slots toward a shard come first; some pair of shards fills all 128 slots. The numbers of used slots from one coarse shard toward the fine shards form the same multiset for every coarse shard, and toward one fine shard from the coarse shards the same multiset again. `pair_slots`: pair k of fine shard s (its fine rows 2 k and 2 k + 1) receives from slot d * 128 + t of coarse shard d's block toward s, the slot that holds its coarse node; each used slot serves exactly one pair.
All inputs are finite; a program needn't handle non-finite values.
Results may differ from a plain program's by a relative error of at most 0.0062.
The roundings to bfloat16 on the way count: a program that leaves them out, or rounds other values in their place, can miss the bound.
Values may be sent and summed in bfloat16 or wider, within the bound.
No kernel may reach another device: no remote copies, remote signals or barrier semaphores. Data moves between devices by JAX's collectives and lax.ppermute only.
A program may use at most 64 MiB of HBM per device.

v0:
```python
import functools
import math

import jax
import jax.numpy as jnp
from jax import lax
from jax.experimental import pallas as pl
from jax.experimental.pallas import tpu as pltpu
from jax.sharding import PartitionSpec as P

HB = 256
LANES = 128
SPAN = 256
EXTRA = 16
TILE = 512
GROUP = 4
SENDERS = 3

F32 = jnp.float32
BF16 = jnp.bfloat16
NT = (((1,), (1,)), ((), ()))
TN = (((0,), (0,)), ((), ()))


def dot(left, right, dims=(((1,), (0,)), ((), ()))):
    return lax.dot_general(left, right, dims, preferred_element_type=F32)


def silu_slope(values):
    sigm = jax.nn.sigmoid(values)
    return sigm * (1.0 + values * (1.0 - sigm))


def columns(row):
    return jnp.broadcast_to(row, (LANES, LANES)).T


def index_columns(ref, first, count):
    return jnp.concatenate([columns(ref[pl.ds(first + i, 1), :]) for i in range(count)], axis=0)


def small(values):
    return values.astype(F32).astype(BF16)


def place_hot(cols):
    place = small(cols & (SPAN - 1))
    lane = lax.broadcasted_iota(jnp.int32, place.shape, 1)
    one, zero = jnp.ones((), BF16), jnp.zeros((), BF16)
    return jnp.concatenate(
        [jnp.where(place == small(lane + start), one, zero) for start in range(0, SPAN, LANES)],
        axis=1,
    )


def gather_rows(hot, block, table, width):
    total = table.shape[1]
    step = max(width, 2 * LANES)
    found = [jnp.zeros(block.shape, F32) for _ in range(width // LANES)]
    for start in range(0, total, step):
        part = dot(hot, table[:, start : start + step])
        for inner in range(0, step, width):
            here = block == (start + inner) // width
            for i in range(len(found)):
                at = inner + i * LANES
                found[i] = jnp.where(here, part[:, at : at + LANES], found[i])
    return found


def spread_rows(hot, block, blocks, values):
    if blocks == 1:
        return [dot(hot, values)]
    parts = []
    zero = jnp.zeros((), BF16)
    for start in range(0, blocks, 2):
        some = range(start, min(start + 2, blocks))
        spread = [jnp.where(block == jnp.full((), j, BF16), values, zero) for j in some]
        part = dot(hot, jnp.concatenate(spread, axis=1))
        parts += [part[:, i * LANES : (i + 1) * LANES] for i in range(len(some))]
    return parts


def add_parts(total, base, parts):
    for j, part in enumerate(parts):
        total[block_rows(base, j), :] += part


def place_hot_rows(ordered, at, tile, base, level):
    one, zero = jnp.ones((), BF16), jnp.zeros((), BF16)
    hot = []
    for i in range(TILE // LANES):
        row = ordered[at, pl.ds(tile * (TILE // LANES) + i, 1), :] - base
        hot.append(jnp.where(level == small(row & (SPAN - 1)), one, zero))
    return jnp.concatenate(hot, axis=1)


def levels():
    return small(lax.broadcasted_iota(jnp.int32, (SPAN, LANES), 0))


def two_parts(values):
    high = values.astype(BF16)
    return high, (values - high.astype(F32)).astype(BF16)


def back(values, weight):
    high, low = two_parts(values)
    return dot(high, weight, NT) + dot(low, weight, NT)


def outer(rows, values):
    high, low = two_parts(values)
    both = dot(rows, jnp.concatenate([high, low], axis=1), TN)
    return both[:, 0:LANES] + both[:, LANES:]


def fetch(sources, targets, arrivals):
    copies = [
        pltpu.make_async_copy(source, target, arrivals.at[i])
        for i, (source, target) in enumerate(zip(sources, targets))
    ]
    for copy in copies:
        copy.start()
    return copies


def coarse_kernel(
    peers,
    latent_ref,
    grad_ref,
    weights_ref,
    rows_ref,
    w_in_ref,
    w_out_ref,
    gain_ref,
    sent_ref,
    table_ref,
    *held,
):
    *held, arrivals = held
    sources = (latent_ref, grad_ref, weights_ref, rows_ref, w_in_ref, w_out_ref, gain_ref)
    copies = fetch(sources, held, arrivals)
    for copy in copies:
        copy.wait()
    latent_ref, grad_ref, weights_ref, rows_ref, w_in_ref, w_out_ref, gain_ref = held
    count = latent_ref.shape[0]
    chunk = SPAN // peers
    capacity = sent_ref.shape[1] - EXTRA - max(EXTRA, chunk)
    w_in, w_out, gain = w_in_ref[...], w_out_ref[...], gain_ref[...]
    latent = latent_ref[...]
    pre = dot(latent, w_in)
    sigm = jax.nn.sigmoid(pre)
    hidden = (pre * sigm).astype(BF16)
    slope = sigm * (1.0 + pre * (1.0 - sigm))
    mapped = dot(hidden, w_out)
    centred = mapped - jnp.mean(mapped, axis=1, keepdims=True)
    inverse = lax.rsqrt(jnp.mean(centred * centred, axis=1, keepdims=True) + 1e-05)
    normed = centred * inverse
    upstream = grad_ref[...].astype(F32)
    scaled = upstream * gain
    grad_mapped = (
        inverse
        * (
            scaled
            - jnp.mean(scaled, axis=1, keepdims=True)
            - normed * jnp.mean(scaled * normed, axis=1, keepdims=True)
        )
    ).astype(BF16)
    grad_pre = (dot(grad_mapped, w_out, NT) * slope).astype(BF16)
    grad_in = (upstream + dot(grad_pre, w_in, NT)).astype(BF16)
    term_gain = jnp.sum(upstream * normed, axis=0, keepdims=True)
    term_in = dot(latent, grad_pre, TN)
    term_out = dot(hidden, grad_mapped, TN)
    for block in range(count // SPAN):
        at = block * SPAN
        table_ref[:, at : at + LANES] = grad_in[at : at + SPAN]
        for half in range(SPAN // LANES):
            at = block * SPAN + half * LANES
            pair = weights_ref[:, at : at + LANES].astype(F32)
            square = jnp.concatenate([pair, jnp.zeros((LANES - 2, LANES), F32)], axis=0)
            table_ref[
                half * LANES : (half + 1) * LANES, block * SPAN + LANES : (block + 1) * SPAN
            ] = square.T.astype(BF16)
    gain_high, gain_low = two_parts(term_gain)
    gain_rows = jnp.concatenate([gain_high.astype(F32), gain_low.astype(F32)], axis=0)
    terms = jnp.concatenate([term_in, term_out], axis=0)
    per_step = 256 // LANES
    for first in range(0, rows_ref.shape[0], per_step):
        cols = index_columns(rows_ref, first, per_step)
        sent, weight = gather_rows(place_hot(cols), cols // SPAN, table_ref, SPAN)
        for part in range(per_step * LANES // capacity):
            peer = first * LANES // capacity + part
            rows = slice(part * capacity, (part + 1) * capacity)
            sent_ref[peer, 0:capacity, :] = sent[rows].astype(BF16)
            square = weight[rows]
            if capacity < LANES:
                square = jnp.concatenate(
                    [square, jnp.zeros((LANES - capacity, LANES), F32)], axis=0
                )
            extra = jnp.concatenate(
                [square.T[0:2], gain_rows, jnp.zeros((EXTRA - 4, LANES), F32)], axis=0
            )
            sent_ref[peer, capacity : capacity + EXTRA, :] = extra.astype(BF16)
            first_row = (peer % 2 * (peers // 2) + peer // 2) * chunk
            share = terms[first_row : first_row + chunk]
            if chunk < EXTRA:
                share = jnp.concatenate([share, jnp.zeros((EXTRA - chunk, LANES), F32)], axis=0)
            sent_ref[peer, capacity + EXTRA :, :] = share.astype(BF16)


def order_edges(recv_ref, off_ref, ordered, stats_vmem, fine_count):
    rows = recv_ref.shape[0]
    shift = (fine_count // LANES).bit_length() - 1
    lane = lax.broadcasted_iota(jnp.int32, (LANES, LANES), 1)
    sub = lax.broadcasted_iota(jnp.int32, (LANES, LANES), 0)
    level = small(sub)
    one, zero = jnp.ones((), BF16), jnp.zeros((), BF16)

    def hot(row):
        return jnp.where(level == small(row), one, zero)

    number = jnp.zeros((LANES, LANES), BF16)
    for row in range(rows):
        number += hot(recv_ref[row : row + 1, :] >> shift)
    ones = jnp.ones((LANES, LANES), BF16)
    total = dot(number, ones)
    high = jnp.floor(total * (1.0 / 64.0))
    low = total - 64.0 * high
    before = jnp.where(lane < sub, 1.0, 0.0).astype(BF16)
    start = 64.0 * dot(before, high.astype(BF16)) + dot(before, low.astype(BF16))
    after = jnp.where(sub < lane, 1.0, 0.0).astype(BF16)
    prefix = jnp.concatenate([after, ones], axis=1)
    positions = []
    filled = start
    for row in range(rows):
        bucket = recv_ref[row : row + 1, :] >> shift
        found = dot(hot(bucket), prefix)
        mine = jnp.where(sub == bucket, found[:, 0:LANES] + filled, 0.0)
        positions.append(jnp.sum(mine, axis=0, keepdims=True).astype(jnp.int32))
        filled = filled + found[:, LANES:]
    moved = jnp.zeros((192, LANES), F32)
    for part in range(0, rows, 4):
        left, right = [], []
        for row in range(part, part + 4):
            position = positions[row]
            recv = recv_ref[row : row + 1, :]
            off = off_ref[row : row + 1, :] + HB
            rest = ((recv >> 8) << 2) | (off >> 8)
            here = level[0:64] == small(position >> 7)
            values = [small(value) for value in (recv & 255, off & 255, rest)]
            left.append(jnp.concatenate([jnp.where(here, v, zero) for v in values], axis=0))
            right.append(hot(position & 127))
        moved += dot(jnp.concatenate(left, axis=1), jnp.concatenate(right, axis=1), NT)
    moved = moved.astype(jnp.int32)
    rest = moved[LANES : LANES + rows]
    recv = moved[0:rows] + ((rest >> 2) << 8)
    send = recv + moved[64 : 64 + rows] + ((rest & 3) << 8)
    ordered[0] = recv
    ordered[1] = send
    lane = lax.broadcasted_iota(jnp.int32, (rows, LANES), 1)
    recv, send = recv.astype(F32), send.astype(F32)
    stats = jnp.where(
        lane < 2,
        jnp.where(
            lane == 0,
            jnp.min(recv, axis=1, keepdims=True),
            jnp.max(recv, axis=1, keepdims=True),
        ),
        jnp.where(
            lane == 2,
            jnp.min(send, axis=1, keepdims=True),
            jnp.max(send, axis=1, keepdims=True),
        ),
    )
    stats_vmem[...] = stats.astype(jnp.int32)


def tile_bases(stats, tile, fine_count):
    count = TILE // LANES
    rows = [tile * count + i for i in range(count)]

    def extreme(pick, at):
        value = stats[rows[0], at]
        for row in rows[1:]:
            value = pick(value, stats[row, at])
        return value

    recv_base = jnp.minimum((extreme(jnp.minimum, 0) >> 4) << 4, fine_count - SPAN)
    send_base = jnp.minimum(
        (extreme(jnp.minimum, 2) >> 4) << 4, fine_count + 2 * HB - SENDERS * SPAN
    )
    fits = (extreme(jnp.maximum, 1) - recv_base < SPAN) & (
        extreme(jnp.maximum, 3) - send_base < SENDERS * SPAN
    )
    return recv_base, send_base, fits


def each_group(step, stats, fine_count, near, far):
    tiles = [step * GROUP + i for i in range(GROUP)]
    places = [tile_bases(stats, tile, fine_count) for tile in tiles]
    fits = functools.reduce(jnp.logical_and, [place[2] for place in places])

    @pl.when(fits)
    def _():
        near(tiles, [place[:2] for place in places])

    @pl.when(jnp.logical_not(fits))
    def _():
        def one(i, carry):
            far(step * GROUP + i)
            return carry

        lax.fori_loop(0, GROUP, one, 0)


def block_rows(base, block):
    return pl.ds(pl.multiple_of(base + block * SPAN, 16), SPAN)


def gather_blocks(hot, block, table, base, blocks):
    found = None
    for start in range(0, blocks, 2):
        some = range(start, min(start + 2, blocks))
        part = dot(hot, jnp.concatenate([table[block_rows(base, j), :] for j in some], axis=1))
        for i, j in enumerate(some):
            one = part[:, i * LANES : (i + 1) * LANES]
            found = one if found is None else jnp.where(block == j, one, found)
    return found


def tile_rows(tile):
    return pl.ds(pl.multiple_of(tile * TILE, TILE), TILE)


def slope_kernel(
    recv_hbm,
    off_hbm,
    slots_hbm,
    fine_hbm,
    weight_hbm,
    first_hbm,
    second_hbm,
    slope_hbm,
    hot_hbm,
    block_hbm,
    window_hbm,
    slope_sum,
    ordered,
    stats_vmem,
    slot_hot,
    slot_block,
    recv_ref,
    off_ref,
    slots_ref,
    window,
    weight_ref,
    halos,
    slope_ref,
    hot_ref,
    block_ref,
    stats,
    arrivals,
    stats_done,
    leaving,
    window_left,
):
    fine_count = fine_hbm.shape[0]
    copies = fetch(
        (recv_hbm, off_hbm, slots_hbm, fine_hbm, weight_hbm, first_hbm, second_hbm),
        (
            recv_ref,
            off_ref,
            slots_ref,
            window.at[pl.ds(HB, fine_count)],
            weight_ref,
            halos.at[0],
            halos.at[1],
        ),
        arrivals,
    )
    copies[0].wait()
    copies[1].wait()
    order_edges(recv_ref, off_ref, ordered, stats_vmem, fine_count)
    stats_copy = pltpu.make_async_copy(stats_vmem, stats, stats_done)
    stats_copy.start()
    for copy in copies[2:]:
        copy.wait()
    slope_sum[...] = jnp.zeros(slope_sum.shape, F32)
    slots = index_columns(slots_ref, 0, slots_ref.shape[0])
    slot_hot[...] = place_hot(slots)
    slot_block[...] = slots // SPAN
    odd = lax.axis_index("curve") & 1
    window[0:HB, :] = halos[1 - odd]
    window[HB + fine_count :, :] = halos[odd]
    window_copy = pltpu.make_async_copy(window, window_hbm, window_left)
    window_copy.start()
    stats_copy.wait()
    count = TILE // LANES
    weight = weight_ref[...]
    level = levels()

    def leave(tile):
        rows = tile_rows(tile)
        pairs = ((slope_ref, slope_hbm), (hot_ref, hot_hbm), (block_ref, block_hbm))
        return [
            pltpu.make_async_copy(source.at[rows], target.at[rows], leaving.at[i, tile])
            for i, (source, target) in enumerate(pairs)
        ]

    def near(tiles, places):
        work = []
        for tile, (recv_base, send_base) in zip(tiles, places):
            recv = index_columns(ordered.at[0], tile * count, count) - recv_base
            send = index_columns(ordered.at[1], tile * count, count) - send_base
            block = send >> 8
            hot = place_hot(recv)
            hot_ref[tile_rows(tile), :] = hot
            block_ref[tile_rows(tile), :] = small(block)
            sender = gather_blocks(place_hot(send), block, window, send_base, SENDERS)
            receiver = gather_blocks(hot, None, window, recv_base + HB, 1)
            work.append((sender, receiver))
        slopes = []
        for tile in tiles:
            for copy in leave(tile)[1:]:
                copy.start()
        for tile, (sender, receiver) in zip(tiles, work):
            inputs = jnp.concatenate([sender.astype(BF16), receiver.astype(BF16)], axis=1)
            slope = silu_slope(dot(inputs, weight))
            slope_ref[tile_rows(tile), :] = slope
            leave(tile)[0].start()
            slopes.append(jnp.concatenate(two_parts(slope), axis=1))
        sums = []
        for tile, (recv_base, _), slope in zip(tiles, places, slopes):
            hot = place_hot_rows(ordered, 0, tile, recv_base, level)
            both = dot(hot, slope)
            sums.append(both[:, 0:LANES] + both[:, LANES:])
        for (recv_base, _), part in zip(places, sums):
            add_parts(slope_sum, recv_base, [part])

    def far(tile):
        recv = index_columns(ordered.at[0], tile * count, count)
        send = index_columns(ordered.at[1], tile * count, count)
        blocks = fine_count // SPAN
        sender = gather_blocks(place_hot(send), send >> 8, window, 0, blocks + 2)
        receiver = gather_blocks(place_hot(recv), recv >> 8, window, HB, blocks)
        inputs = jnp.concatenate([sender.astype(BF16), receiver.astype(BF16)], axis=1)
        slope = silu_slope(dot(inputs, weight))
        slope_ref[tile_rows(tile), :] = slope
        hot = place_hot_rows(ordered, 0, tile, 0, level)
        for part in two_parts(slope):
            add_parts(slope_sum, 0, spread_rows(hot, small(recv >> 8), blocks, part))
        hot_ref[tile_rows(tile), :] = jnp.zeros((TILE, SPAN), BF16)
        block_ref[tile_rows(tile), :] = jnp.zeros((TILE, LANES), BF16)
        for copy in leave(tile):
            copy.start()

    def step(index, carry):
        each_group(index, stats, fine_count, near, far)
        return carry

    tiles = slope_ref.shape[0] // TILE
    lax.fori_loop(0, tiles // GROUP, step, 0)
    window_copy.wait()
    for tile in range(tiles):
        for copy in leave(tile):
            copy.wait()


def edge_kernel(
    coarse_scale,
    stats,
    arrived_hbm,
    slot_hot_hbm,
    slot_block_hbm,
    hot_hbm,
    slope_hbm,
    block_hbm,
    ordered_hbm,
    window_hbm,
    slope_sum_hbm,
    weight_hbm,
    grad_table,
    send_sum,
    first_ref,
    second_ref,
    keep_ref,
    gain_ref,
    slot_table,
    grad_rows,
    arrived_ref,
    slot_hot,
    slot_block,
    hot_ref,
    slope_ref,
    block_ref,
    ordered,
    window,
    slope_sum,
    weight_ref,
    arrivals,
):
    fine_count = grad_table.shape[0]
    copies = fetch(
        (
            arrived_hbm,
            slot_hot_hbm,
            slot_block_hbm,
            hot_hbm,
            slope_hbm,
            block_hbm,
            ordered_hbm,
            window_hbm,
            slope_sum_hbm,
            weight_hbm,
        ),
        (
            arrived_ref,
            slot_hot,
            slot_block,
            hot_ref,
            slope_ref,
            block_ref,
            ordered,
            window,
            slope_sum,
            weight_ref,
        ),
        arrivals,
    )
    send_sum[...] = jnp.zeros(send_sum.shape, F32)
    peers = arrived_ref.shape[0]
    share = max(EXTRA, SPAN // peers)
    capacity = arrived_ref.shape[1] - EXTRA - share
    per_block = SPAN // capacity
    for copy in copies[:3]:
        copy.wait()
    coarse = jnp.zeros((share, LANES), F32)
    gain = jnp.zeros((1, LANES), F32)
    for peer in range(peers):
        block, part = divmod(peer, per_block)
        rows = slice(part * capacity, (part + 1) * capacity)
        slot_table[rows, block * SPAN : block * SPAN + LANES] = arrived_ref[peer, 0:capacity, :]
        extra = arrived_ref[peer, capacity : capacity + EXTRA, :].astype(F32)
        square = jnp.concatenate([extra, jnp.zeros((LANES - EXTRA, LANES), F32)], axis=0).T
        slot_table[rows, block * SPAN + LANES : (block + 1) * SPAN] = square[0:capacity].astype(
            BF16
        )
        gain += extra[2:3] + extra[3:4]
        coarse += arrived_ref[peer, capacity + EXTRA :, :].astype(F32)
    keep_ref[LANES:, :] = coarse
    gain_ref[...] = gain * coarse_scale

    found = []
    for first in range(0, slot_hot.shape[0], SPAN):
        at = slice(first, first + SPAN)
        found.append(gather_rows(slot_hot[at, :], slot_block[at, :], slot_table, SPAN))
    for i, (grad, weight) in enumerate(found):
        first = i * SPAN
        for r in range(2):
            rows = (grad * weight[:, r : r + 1]).astype(BF16).astype(F32)
            grad_rows[pl.ds(2 * first + r, SPAN, stride=2), :] = rows
    grad_table[...] = grad_rows[...].astype(BF16)
    for copy in copies[3:]:
        copy.wait()

    count = TILE // LANES
    level = levels()

    def near(tiles, places):
        work = []
        for tile, (recv_base, _) in zip(tiles, places):
            rows = tile_rows(tile)
            upstream = gather_blocks(hot_ref[rows, :], None, grad_table, recv_base, 1)
            work.append((upstream * slope_ref[rows, :]).astype(BF16))
        sums = []
        for tile, (_, send_base), values in zip(tiles, places, work):
            hot = place_hot_rows(ordered, 1, tile, send_base, level)
            sums.append(spread_rows(hot, block_ref[tile_rows(tile), :], SENDERS, values))
        for (_, send_base), parts in zip(places, sums):
            add_parts(send_sum, send_base, parts)

    def far(tile):
        rows = tile_rows(tile)
        recv = index_columns(ordered.at[0], tile * count, count)
        send = index_columns(ordered.at[1], tile * count, count)
        blocks = fine_count // SPAN
        upstream = gather_blocks(place_hot(recv), recv >> 8, grad_table, 0, blocks)
        values = (upstream * slope_ref[rows, :]).astype(BF16)
        hot = place_hot_rows(ordered, 1, tile, 0, level)
        add_parts(send_sum, 0, spread_rows(hot, small(send >> 8), blocks + 2, values))

    def step(index, carry):
        each_group(index, stats, fine_count, near, far)
        return carry

    lax.fori_loop(0, slope_ref.shape[0] // TILE // GROUP, step, 0)

    weight_send = weight_ref[0:LANES, :]
    odd = lax.axis_index("curve") & 1
    to_prev = back(send_sum[0:HB, :], weight_send)
    to_next = back(send_sum[HB + fine_count :, :], weight_send)
    first_ref[LANES:, :] = jnp.where(odd == 0, to_next, to_prev).astype(BF16)
    second_ref[...] = jnp.where(odd == 0, to_prev, to_next).astype(BF16)
    term_send = jnp.zeros((LANES, LANES), F32)
    term_recv = jnp.zeros((LANES, LANES), F32)
    for first in range(0, fine_count + 2 * HB, SPAN):
        at = slice(first, first + SPAN)
        term_send += outer(window[at, :], send_sum[at, :])
    for first in range(0, fine_count, SPAN):
        at = slice(first, first + SPAN)
        moved = slice(HB + first, HB + first + SPAN)
        term_recv += outer(window[moved, :], grad_rows[at, :] * slope_sum[at, :])
    keep_ref[0:LANES, :] = jnp.where(odd == 0, term_send, term_recv)
    first_ref[0:LANES, :] = jnp.where(odd == 0, term_recv, term_send).astype(BF16)


def fine_kernel(
    grad_hbm,
    send_sum_hbm,
    slope_sum_hbm,
    weight_hbm,
    first_hbm,
    second_hbm,
    fine_ref,
    grad_table,
    send_sum,
    slope_sum,
    weight_ref,
    first_ref,
    second_ref,
    arrivals,
):
    fine_count = fine_ref.shape[0]
    for copy in fetch(
        (grad_hbm, send_sum_hbm, slope_sum_hbm, weight_hbm, first_hbm, second_hbm),
        (grad_table, send_sum, slope_sum, weight_ref, first_ref, second_ref),
        arrivals,
    ):
        copy.wait()
    odd = lax.axis_index("curve") & 1
    one, two = first_ref[LANES:, :].astype(F32), second_ref[...].astype(F32)
    from_next, from_prev = jnp.where(odd == 0, one, two), jnp.where(odd == 0, two, one)
    for first in range(0, fine_count, SPAN):
        at = slice(first, first + SPAN)
        moved = slice(HB + first, HB + first + SPAN)
        grad = grad_table[at, :].astype(F32)
        summed = (
            grad
            + back(send_sum[moved, :], weight_ref[0:LANES, :])
            + back(grad * slope_sum[at, :], weight_ref[LANES:, :])
        )
        if first == 0:
            summed += from_prev
        if first == fine_count - SPAN:
            summed += from_next
        fine_ref[at, :] = summed.astype(BF16)


def last_kernel(
    edge_scale, coarse_scale, own_ref, coarse_ref, there_ref, edge_ref, in_ref, out_ref
):
    odd = lax.axis_index("curve") & 1
    own, coarse = own_ref[...], coarse_ref[...].astype(F32)
    other, other_coarse = there_ref[0:LANES, :], there_ref[LANES:, :]
    edge_ref[0:LANES, :] = jnp.where(odd == 0, own, other) * edge_scale
    edge_ref[LANES:, :] = jnp.where(odd == 0, other, own) * edge_scale
    in_ref[...] = jnp.where(odd == 0, coarse, other_coarse) * coarse_scale
    out_ref[...] = jnp.where(odd == 0, other_coarse, coarse) * coarse_scale


def pair_exchange(first, second, peers):
    pairs = [(i, i ^ 1) for i in range(peers)]
    between = [(i, ((i + 1) ^ 1) - 1) for i in range(1, peers - 1)]
    return lax.ppermute(first, "curve", pairs), lax.ppermute(second, "curve", between)


def joined(later, own, there):
    return jnp.where(
        later, jnp.concatenate([there, own], axis=0), jnp.concatenate([own, there], axis=0)
    )


def swapped(values, hops, peers):
    return lax.ppermute(values, "curve", [(i, i ^ hops) for i in range(peers)])


def reduced(sent, half, device, peers, beside):
    hops = 2
    while hops < peers // 4:
        there = swapped(sent, hops, peers)
        own = sent[:half].astype(F32) + there[:half].astype(F32)
        coarse = joined((device & hops) != 0, sent[half:], there[half:])
        sent = jnp.concatenate([own.astype(BF16), coarse], axis=0)
        hops *= 2
    near, far = peers // 4, peers // 2
    parts = [sent] + [swapped(sent, hops, peers) for hops in (near, far, near + far)]
    *parts, beside = lax.optimization_barrier((*parts, beside))
    sums = [part[:half].astype(F32) for part in parts]
    rows = [part[half:] for part in parts]
    own = (sums[0] + sums[1]) + (sums[2] + sums[3])
    later = (device & near) != 0
    coarse = joined(
        (device & far) != 0, joined(later, rows[0], rows[1]), joined(later, rows[2], rows[3])
    )
    return own, coarse, beside


def per_device(
    fine_latent,
    coarse_latent,
    grad_coarse,
    restrict_weights,
    send_rows,
    pair_slots,
    edge_receivers,
    edge_offsets,
    edge_weight,
    node_weight_in,
    node_weight_out,
    node_gain,
):
    peers = lax.axis_size("curve")
    device = lax.axis_index("curve")
    even = (device & 1) == 0
    coarse_count = coarse_latent.shape[0]
    fine_count = fine_latent.shape[0]
    edge_count = edge_receivers.shape[0]
    capacity = send_rows.shape[0] // peers
    chunk = SPAN // peers
    share = max(EXTRA, chunk)
    payload = capacity + EXTRA + share
    edge_rows = edge_count // LANES
    window_count = fine_count + 2 * HB
    params = pltpu.CompilerParams(vmem_limit_bytes=64 * 1024 * 1024 - 256 * 1024)
    roomy = pltpu.CompilerParams(vmem_limit_bytes=62 * 1024 * 1024)
    anywhere = pl.BlockSpec(memory_space=pl.ANY)

    scalar = pl.BlockSpec(memory_space=pltpu.SMEM)

    head, end = fine_latent[:HB], fine_latent[fine_count - HB :]
    halos = pair_exchange(jnp.where(even, end, head), jnp.where(even, head, end), peers)

    sent = pl.pallas_call(
        functools.partial(coarse_kernel, peers),
        out_shape=jax.ShapeDtypeStruct((peers, payload, LANES), BF16),
        in_specs=[anywhere] * 7,
        scratch_shapes=[
            pltpu.VMEM((SPAN, coarse_count), BF16),
            pltpu.VMEM((coarse_count, LANES), BF16),
            pltpu.VMEM((coarse_count, LANES), BF16),
            pltpu.VMEM((2, coarse_count), BF16),
            pltpu.VMEM((peers * capacity // LANES, LANES), jnp.int32),
            pltpu.VMEM((LANES, LANES), BF16),
            pltpu.VMEM((LANES, LANES), BF16),
            pltpu.VMEM((1, LANES), F32),
            pltpu.SemaphoreType.DMA((7,)),
        ],
        compiler_params=params,
        cost_estimate=pl.CostEstimate(
            flops=2_000_000_000, bytes_accessed=2_000_000, transcendentals=400_000
        ),
        name="coarse_block",
    )(
        coarse_latent,
        grad_coarse,
        restrict_weights,
        send_rows.reshape(-1, LANES),
        node_weight_in,
        node_weight_out,
        node_gain.reshape(1, LANES),
    )
    arrived = lax.all_to_all(sent, "curve", split_axis=0, concat_axis=0, tiled=True)

    pair_count = fine_count // 2
    in_vmem = pl.BlockSpec(memory_space=pltpu.VMEM)
    slope, hot, block, window, slope_sum, ordered, stats, slot_hot, slot_block = pl.pallas_call(
        slope_kernel,
        out_shape=(
            jax.ShapeDtypeStruct((edge_count, LANES), F32),
            jax.ShapeDtypeStruct((edge_count, SPAN), BF16),
            jax.ShapeDtypeStruct((edge_count, LANES), BF16),
            jax.ShapeDtypeStruct((window_count, LANES), BF16),
            jax.ShapeDtypeStruct((fine_count, LANES), F32),
            jax.ShapeDtypeStruct((2, edge_rows, LANES), jnp.int32),
            jax.ShapeDtypeStruct((edge_rows, LANES), jnp.int32),
            jax.ShapeDtypeStruct((pair_count, SPAN), BF16),
            jax.ShapeDtypeStruct((pair_count, LANES), jnp.int32),
        ),
        in_specs=[anywhere] * 7,
        out_specs=[anywhere] * 4 + [in_vmem] * 5,
        scratch_shapes=[
            pltpu.VMEM((edge_rows, LANES), jnp.int32),
            pltpu.VMEM((edge_rows, LANES), jnp.int32),
            pltpu.VMEM((pair_count // LANES, LANES), jnp.int32),
            pltpu.VMEM((window_count, LANES), BF16),
            pltpu.VMEM((2 * LANES, LANES), BF16),
            pltpu.VMEM((2, HB, LANES), BF16),
            pltpu.VMEM((edge_count, LANES), F32),
            pltpu.VMEM((edge_count, SPAN), BF16),
            pltpu.VMEM((edge_count, LANES), BF16),
            pltpu.SMEM((edge_rows, LANES), jnp.int32),
            pltpu.SemaphoreType.DMA((7,)),
            pltpu.SemaphoreType.DMA,
            pltpu.SemaphoreType.DMA((3, edge_count // TILE)),
            pltpu.SemaphoreType.DMA,
        ],
        compiler_params=params,
        cost_estimate=pl.CostEstimate(
            flops=16_000_000_000, bytes_accessed=5_000_000, transcendentals=800_000
        ),
        name="edge_slope",
    )(
        edge_receivers.reshape(-1, LANES),
        edge_offsets.reshape(-1, LANES),
        pair_slots.reshape(-1, LANES),
        fine_latent,
        edge_weight,
        *halos,
    )

    coarse_scale = 1.0 / math.sqrt(coarse_count * peers)
    edge_scale = 1.0 / math.sqrt(edge_count * peers)
    grad_rows, send_sum, first, second, keep, term_gain = pl.pallas_call(
        functools.partial(edge_kernel, coarse_scale),
        out_shape=(
            jax.ShapeDtypeStruct((fine_count, LANES), BF16),
            jax.ShapeDtypeStruct((window_count, LANES), F32),
            pltpu.VMEM((LANES + HB, LANES), BF16),
            pltpu.VMEM((HB, LANES), BF16),
            pltpu.VMEM((LANES + share, LANES), F32),
            jax.ShapeDtypeStruct((1, LANES), F32),
        ),
        in_specs=[scalar] + [anywhere] * 10,
        scratch_shapes=[
            pltpu.VMEM((SPAN, peers * capacity), BF16),
            pltpu.VMEM((fine_count, LANES), F32),
            pltpu.VMEM((peers, payload, LANES), BF16),
            pltpu.VMEM((pair_count, SPAN), BF16),
            pltpu.VMEM((pair_count, LANES), jnp.int32),
            pltpu.VMEM((edge_count, SPAN), BF16),
            pltpu.VMEM((edge_count, LANES), F32),
            pltpu.VMEM((edge_count, LANES), BF16),
            pltpu.VMEM((2, edge_rows, LANES), jnp.int32),
            pltpu.VMEM((window_count, LANES), BF16),
            pltpu.VMEM((fine_count, LANES), F32),
            pltpu.VMEM((2 * LANES, LANES), BF16),
            pltpu.SemaphoreType.DMA((10,)),
        ],
        compiler_params=roomy,
        cost_estimate=pl.CostEstimate(
            flops=24_000_000_000, bytes_accessed=8_000_000, transcendentals=0
        ),
        name="edge_back",
    )(
        stats,
        arrived,
        slot_hot,
        slot_block,
        hot,
        slope,
        block,
        ordered,
        window,
        slope_sum,
        edge_weight,
    )
    one, two = pair_exchange(first, second, peers)
    sent = keep[: LANES + chunk] + jnp.pad(one[:LANES].astype(F32), ((0, chunk), (0, 0)))
    sent = sent.astype(BF16)
    grad_fine = pl.pallas_call(
        fine_kernel,
        out_shape=jax.ShapeDtypeStruct((fine_count, LANES), BF16),
        in_specs=[anywhere] * 6,
        scratch_shapes=[
            pltpu.VMEM((fine_count, LANES), BF16),
            pltpu.VMEM((window_count, LANES), F32),
            pltpu.VMEM((fine_count, LANES), F32),
            pltpu.VMEM((2 * LANES, LANES), BF16),
            pltpu.VMEM((LANES + HB, LANES), BF16),
            pltpu.VMEM((HB, LANES), BF16),
            pltpu.SemaphoreType.DMA((6,)),
        ],
        compiler_params=pltpu.CompilerParams(vmem_limit_bytes=64 * 1024 * 1024 - 640 * 1024),
        cost_estimate=pl.CostEstimate(
            flops=1_000_000_000, bytes_accessed=4_000_000, transcendentals=0
        ),
        name="fine_sums",
    )(grad_rows, send_sum, slope_sum, edge_weight, one, two)
    own, coarse, grad_fine = reduced(sent, LANES, device, peers, grad_fine)
    there = swapped(jnp.concatenate([own, coarse.astype(F32)], axis=0), 1, peers)
    edge_terms, term_in, term_out = pl.pallas_call(
        functools.partial(last_kernel, edge_scale, coarse_scale),
        out_shape=(
            jax.ShapeDtypeStruct((2 * LANES, LANES), F32),
            jax.ShapeDtypeStruct((LANES, LANES), F32),
            jax.ShapeDtypeStruct((LANES, LANES), F32),
        ),
        compiler_params=pltpu.CompilerParams(vmem_limit_bytes=4 * 1024 * 1024),
        name="last_terms",
    )(own, coarse, there)
    return grad_fine, edge_terms, term_in, term_out, term_gain.reshape(LANES)


def solution(mesh):
    placed = (
        P(("groups", "curve"), None),
        P(("groups", "curve"), None),
        P(("groups", "curve"), None),
        P(None, ("groups", "curve")),
        P(("groups", "curve")),
        P(("groups", "curve")),
        P(("groups", "curve")),
        P(("groups", "curve")),
        P(),
        P(),
        P(),
        P(),
    )
    return jax.shard_map(
        per_device,
        mesh=mesh,
        in_specs=placed,
        out_specs=(
            P(("groups", "curve"), None),
            P("groups", None),
            P("groups", None),
            P("groups", None),
            P("groups"),
        ),
        check_vma=False,
    )
```

profile of v0, /device:TPU:0, one launch (start us, length us, event | category | flops | bytes accessed | tf_op | source)
XLA Modules:
  0.0 61.1 jit_solution(14239374310865590891)
XLA Ops:
  0.6 0.9 %broadcast_select_fusion = (bf16[256,128]{1,0:T(8,128)(2,1)S(1)}, bf16[256,128]{1,0:T(8,128)(2,1)S(1)}) fusion(pred[]{:T(512)S(6)} %eq.3, bf16[2048,128]{1,0:T(8,128)(2,1)} %fine_hbm.1), kind=kLoop, calls=%fused_computation.4 | loop fusion | flops 65536 | bytes 262145 | tf_op jit(solution)/shard_map/jit(_where)/select_n | solution.py:741
  1.5 0.5 collective-permute-start
  2.0 1.3 %collective-permute-start.1 = (bf16[256,128]{1,0:T(8,128)(2,1)S(1)}, bf16[256,128]{1,0:T(8,128)(2,1)}, u32[]{:S(2)}, u32[]{:S(2)}) collective-permute-start(bf16[256,128]{1,0:T(8,128)(2,1)S(1)} %get-tuple-element.53), channel_id=1, source_target_pairs={{1,2},{2,1},{3,4},{4,3},{5,6},{6,5},{7,8},{8,7},{9,10},{10,9},{11,... | collective-permute-start | bytes 196616 | tf_op jit(solution)/shard_map/ppermute | solution.py:674
  3.3 4.9 %coarse_block.1 = bf16[16,160,128]{2,1,0:T(8,128)(2,1)} custom-call(bf16[1024,128]{1,0:T(8,128)(2,1)} %latent_ref.1, bf16[1024,128]{1,0:T(8,128)(2,1)} %grad_ref.1, bf16[2,1024]{1,0:T(2,128)(2,1)} %weights_ref.1, s32[16,128]{1,0:T(8,128)} %bitcast.8, bf16[128,128]{1,0:T(8,128)(2,1)} %w_in_ref.1, bf16[128,128]{1,0:T(8,128)(2,1)} %w_out_ref.1, f32[1,128]{1,0:T(1,128)} %bitcast.10), custom_call_target="tpu_custom_call" | custom-call | flops 2000000000 | bytes 2000000 | tf_op jit(solution)/shard_map/coarse_block/pallas_call | solution.py:743
  8.2 8.2 %all-to-all-start = ((bf16[16,160,128]{2,1,0:T(8,128)(2,1)}), bf16[16,160,128]{2,1,0:T(8,128)(2,1)}, u32[]{:S(2)}, u32[]{:S(2)}) async-start(bf16[16,160,128]{2,1,0:T(8,128)(2,1)} %coarse_block.1), calls=%async_computation | async-start | bytes 1310720 | tf_op jit(solution)/shard_map/all_to_all | solution.py:772
  16.5 0.6 copy-done.3
  17.1 11.6 %edge_slope.1 = (f32[6144,128]{1,0:T(8,128)}, bf16[6144,256]{1,0:T(8,128)(2,1)}, bf16[6144,128]{1,0:T(8,128)(2,1)}, bf16[2560,128]{1,0:T(8,128)(2,1)}, f32[2048,...) custom-call(s32[48,128]{1,0:T(8,128)} %bitcast.6, ...), custom_call_target="tpu_custom_call" | custom-call | flops 16000000000 | bytes 5000000 | tf_op jit(solution)/shard_map/edge_slope/pallas_call | solution.py:776
  28.7 4.4 %all-to-all-done.arrived_hbm = bf16[16,160,128]{2,1,0:T(8,128)(2,1)} async-done(((bf16[16,160,128]{2,1,0:T(8,128)(2,1)}), bf16[16,160,128]{2,1,0:T(8,128)(2,1)}, u32[]{:S(2)}, u32[]{:S(2)}) %all-to-all-start) | async-done | bytes 655392 | tf_op jit(solution)/shard_map/all_to_all | solution.py:772
  33.1 10.5 %edge_back.1 = (bf16[2048,128]{1,0:T(8,128)(2,1)}, f32[2560,128]{1,0:T(8,128)}, bf16[384,128]{1,0:T(8,128)(2,1)S(1)}, bf16[256,128]{1,0:T(8,128)(2,1)S(1)}, f32[144,128]{1,0:T(8,128)S(1)}, /*index=5*/f32[1,128]{1,0:T(1,128)}) custom-call(s32[48,128]{1,0:T(8,128)} %get-tuple-element.28.stats, bf16[16,160,128]{2,1,0:T(8,128)(2,1)} %all-to-all-done.arrived_hbm, ...), custom_call_target="tpu_custom_call" | custom-call | flops 24000000000 | bytes 8000000 | tf_op jit(solution)/shard_map/edge_back/pallas_call | solution.py:823
  43.6 0.1 collective-permute-start.2
  43.8 1.2 %collective-permute-done.2.first_hbm = bf16[384,128]{1,0:T(8,128)(2,1)S(1)} collective-permute-done((bf16[384,128]{1,0:T(8,128)(2,1)S(1)}, bf16[384,128]{1,0:T(8,128)(2,1)S(1)}, u32[]{:S(2)}, u32[]{:S(2)}) %collective-permute-start.2) | collective-permute-done | bytes 98336 | tf_op jit(solution)/shard_map/ppermute | solution.py:674
  45.0 0.1 add_convert_fusion
  45.1 1.2 %collective-permute-start.3 = (bf16[144,128]{1,0:T(8,128)(2,1)S(1)}, bf16[144,128]{1,0:T(8,128)(2,1)S(1)}, u32[]{:S(2)}, u32[]{:S(2)}) collective-permute-start(bf16[144,128]{1,0:T(8,128)(2,1)S(1)} %add_convert_fusion), channel_id=1, source_target_pairs={{0,2},{1,3},{2,0},{3,1},{4,6},{5,7},{6,4},{7,5},{8,10},{9,11},{10,... | collective-permute-start | bytes 110600 | tf_op jit(solution)/shard_map/ppermute | solution.py:684
  46.3 0.7 %collective-permute-start.7 = (bf16[256,128]{1,0:T(8,128)(2,1)S(1)}, bf16[256,128]{1,0:T(8,128)(2,1)S(1)}, u32[]{:S(2)}, u32[]{:S(2)}) collective-permute-start(bf16[256,128]{1,0:T(8,128)(2,1)S(1)} %get-tuple-element.41), channel_id=1, source_target_pairs={{1,2},{2,1},{3,4},{4,3},{5,6},{6,5},{7,8},{8,7},{9,10},{10,9},{11,... | collective-permute-start | bytes 196616 | tf_op jit(solution)/shard_map/ppermute | solution.py:674
  47.0 2.2 %collective-permute-done.3 = bf16[144,128]{1,0:T(8,128)(2,1)S(1)} collective-permute-done((bf16[144,128]{1,0:T(8,128)(2,1)S(1)}, bf16[144,128]{1,0:T(8,128)(2,1)S(1)}, u32[]{:S(2)}, u32[]{:S(2)}) %collective-permute-start.3) | collective-permute-done | bytes 36896 | tf_op jit(solution)/shard_map/ppermute | solution.py:684
  49.2 2.1 %collective-permute-start.4 = (bf16[160,128]{1,0:T(8,128)(2,1)S(1)}, bf16[160,128]{1,0:T(8,128)(2,1)S(1)}, u32[]{:S(2)}, u32[]{:S(2)}) collective-permute-start(bf16[160,128]{1,0:T(8,128)(2,1)S(1)} %pad_maximum_fusion.1), channel_id=1, source_target_pairs={{0,4},{1,5},{2,6},{3,7},{4,0},{5,1},{6,2},{7,3},{8,12},{9,13},{10,... | collective-permute-start | bytes 122888 | tf_op jit(solution)/shard_map/ppermute | solution.py:684
  51.2 1.9 %collective-permute-start.5 = (bf16[160,128]{1,0:T(8,128)(2,1)S(1)}, bf16[160,128]{1,0:T(8,128)(2,1)S(1)}, u32[]{:S(2)}, u32[]{:S(2)}) collective-permute-start(bf16[160,128]{1,0:T(8,128)(2,1)S(1)} %pad_maximum_fusion.1), channel_id=1, source_target_pairs={{0,8},{1,9},{2,10},{3,11},{4,12},{5,13},{6,14},{7,15},{8,0},{9,1},... | collective-permute-start | bytes 122888 | tf_op jit(solution)/shard_map/ppermute | solution.py:684
  53.1 0.6 collective-permute-start.6
  53.7 0.6 %copy-done.2 = bf16[256,128]{1,0:T(8,128)(2,1)} copy-done((bf16[256,128]{1,0:T(8,128)(2,1)}, bf16[256,128]{1,0:T(8,128)(2,1)S(1)}, u32[]{:S(2)}) %copy-start.2) | copy-done | bytes 65560
  54.3 3.4 %fine_sums.1 = bf16[2048,128]{1,0:T(8,128)(2,1)} custom-call(bf16[2048,128]{1,0:T(8,128)(2,1)} %get-tuple-element.39.grad_hbm, f32[2560,128]{1,0:T(8,128)} %get-tuple-element.40.send_sum_hbm, f32[2048,128]{1,0:T(8,128)} %get-tuple-element.36.slope_sum_hbm, bf16[256,128]{1,0:T(8,128)(2,1)} %weight_hbm.5, bf16[384,128]{1,0:T(8,128)(2,1)} %copy-done, ...), custom_call_target="tpu_custom_call" | custom-call | flops 1000000000 | bytes 4000000 | tf_op jit(solution)/shard_map/fine_sums/pallas_call | solution.py:870
  57.7 1.2 %collective-permute-done.6 = bf16[160,128]{1,0:T(8,128)(2,1)S(1)} collective-permute-done((bf16[160,128]{1,0:T(8,128)(2,1)S(1)}, bf16[160,128]{1,0:T(8,128)(2,1)S(1)}, u32[]{:S(2)}, u32[]{:S(2)}) %collective-permute-start.6) | collective-permute-done | bytes 40992 | tf_op jit(solution)/shard_map/ppermute | solution.py:684
  59.0 0.1 collective-permute-start.8
  59.1 1.3 %collective-permute-done.8.there_ref = f32[256,128]{1,0:T(8,128)S(1)} collective-permute-done((f32[256,128]{1,0:T(8,128)S(1)}, f32[256,128]{1,0:T(8,128)S(1)}, u32[]{:S(2)}, u32[]{:S(2)}) %collective-permute-start.8) | collective-permute-done | bytes 131104 | tf_op jit(solution)/shard_map/ppermute | solution.py:684
  60.4 0.7 %last_terms.1 = (f32[256,128]{1,0:T(8,128)}, f32[128,128]{1,0:T(8,128)}, f32[128,128]{1,0:T(8,128)}) custom-call(f32[128,128]{1,0:T(8,128)S(1)} %add_add_fusion.own_ref, bf16[128,128]{1,0:T(8,128)(2,1)S(1)} %get-tuple-element.52.coarse_ref, f32[256,128]{1,0:T(8,128)S(1)} %collective-permute-done.8.there_ref), custom_call_target="tpu_custom_call" | custom-call | tf_op jit(solution)/shard_map/last_terms/pallas_call | solution.py:891
  (24 shorter events, 0.1 us)
Async XLA Ops:
  1.5 14.9 %collective-permute-start = (bf16[256,128]{1,0:T(8,128)(2,1)S(1)}, bf16[256,128]{1,0:T(8,128)(2,1)S(1)}, u32[]{:S(2)}, u32[]{:S(2)}) collective-permute-start(bf16[256,128]{1,0:T(8,128)(2,1)S(1)} %get-tuple-element.54), channel_id=1, source_target_pairs={{0,1},{1,0},{2,3},{3,2},{4,5},{5,4},{6,7},{7,6},{8,9},{9,8},{10,11... | collective-permute-start | bytes 196616 | tf_op jit(solution)/shard_map/ppermute | solution.py:674
  2.0 14.5 %collective-permute-start.1 = (bf16[256,128]{1,0:T(8,128)(2,1)S(1)}, bf16[256,128]{1,0:T(8,128)(2,1)}, u32[]{:S(2)}, u32[]{:S(2)}) collective-permute-start(bf16[256,128]{1,0:T(8,128)(2,1)S(1)} %get-tuple-element.53), channel_id=1, source_target_pairs={{1,2},{2,1},{3,4},{4,3},{5,6},{6,5},{7,8},{8,7},{9,10},{10,9},{11,... | collective-permute-start | bytes 196616 | tf_op jit(solution)/shard_map/ppermute | solution.py:674
  8.2 24.9 %all-to-all-start = ((bf16[16,160,128]{2,1,0:T(8,128)(2,1)}), bf16[16,160,128]{2,1,0:T(8,128)(2,1)}, u32[]{:S(2)}, u32[]{:S(2)}) async-start(bf16[16,160,128]{2,1,0:T(8,128)(2,1)} %coarse_block.1), calls=%async_computation | async-start | bytes 1310720 | tf_op jit(solution)/shard_map/all_to_all | solution.py:772
  16.5 0.6 %copy-start.3 = (bf16[256,128]{1,0:T(8,128)(2,1)}, bf16[256,128]{1,0:T(8,128)(2,1)S(1)}, u32[]{:S(2)}) copy-start(bf16[256,128]{1,0:T(8,128)(2,1)S(1)} %collective-permute-done.first_hbm) | copy-start | bytes 196612
  33.1 11.9 %copy-start.1 = (pred[144]{0:T(512)(128)(4,1)S(1)}, pred[144]{0:T(512)(128)(4,1)}, u32[]{:S(2)}) copy-start(pred[144]{0:T(512)(128)(4,1)} %constant.14.clone.1) | copy-start | bytes 436
  43.6 1.4 %collective-permute-start.2 = (bf16[384,128]{1,0:T(8,128)(2,1)S(1)}, bf16[384,128]{1,0:T(8,128)(2,1)S(1)}, u32[]{:S(2)}, u32[]{:S(2)}) collective-permute-start(bf16[384,128]{1,0:T(8,128)(2,1)S(1)} %get-tuple-element.38), channel_id=1, source_target_pairs={{0,1},{1,0},{2,3},{3,2},{4,5},{5,4},{6,7},{7,6},{8,9},{9,8},{10,11... | collective-permute-start | bytes 294920 | tf_op jit(solution)/shard_map/ppermute | solution.py:674
  45.0 8.7 %copy-start = (bf16[384,128]{1,0:T(8,128)(2,1)}, bf16[384,128]{1,0:T(8,128)(2,1)S(1)}, u32[]{:S(2)}) copy-start(bf16[384,128]{1,0:T(8,128)(2,1)S(1)} %collective-permute-done.2.first_hbm) | copy-start | bytes 294916
  45.1 4.0 %collective-permute-start.3 = (bf16[144,128]{1,0:T(8,128)(2,1)S(1)}, bf16[144,128]{1,0:T(8,128)(2,1)S(1)}, u32[]{:S(2)}, u32[]{:S(2)}) collective-permute-start(bf16[144,128]{1,0:T(8,128)(2,1)S(1)} %add_convert_fusion), channel_id=1, source_target_pairs={{0,2},{1,3},{2,0},{3,1},{4,6},{5,7},{6,4},{7,5},{8,10},{9,11},{10,... | collective-permute-start | bytes 110600 | tf_op jit(solution)/shard_map/ppermute | solution.py:684
  46.3 7.4 %collective-permute-start.7 = (bf16[256,128]{1,0:T(8,128)(2,1)S(1)}, bf16[256,128]{1,0:T(8,128)(2,1)S(1)}, u32[]{:S(2)}, u32[]{:S(2)}) collective-permute-start(bf16[256,128]{1,0:T(8,128)(2,1)S(1)} %get-tuple-element.41), channel_id=1, source_target_pairs={{1,2},{2,1},{3,4},{4,3},{5,6},{6,5},{7,8},{8,7},{9,10},{10,9},{11,... | collective-permute-start | bytes 196616 | tf_op jit(solution)/shard_map/ppermute | solution.py:674
  49.2 8.5 %collective-permute-start.4 = (bf16[160,128]{1,0:T(8,128)(2,1)S(1)}, bf16[160,128]{1,0:T(8,128)(2,1)S(1)}, u32[]{:S(2)}, u32[]{:S(2)}) collective-permute-start(bf16[160,128]{1,0:T(8,128)(2,1)S(1)} %pad_maximum_fusion.1), channel_id=1, source_target_pairs={{0,4},{1,5},{2,6},{3,7},{4,0},{5,1},{6,2},{7,3},{8,12},{9,13},{10,... | collective-permute-start | bytes 122888 | tf_op jit(solution)/shard_map/ppermute | solution.py:684
  51.2 6.4 %collective-permute-start.5 = (bf16[160,128]{1,0:T(8,128)(2,1)S(1)}, bf16[160,128]{1,0:T(8,128)(2,1)S(1)}, u32[]{:S(2)}, u32[]{:S(2)}) collective-permute-start(bf16[160,128]{1,0:T(8,128)(2,1)S(1)} %pad_maximum_fusion.1), channel_id=1, source_target_pairs={{0,8},{1,9},{2,10},{3,11},{4,12},{5,13},{6,14},{7,15},{8,0},{9,1},... | collective-permute-start | bytes 122888 | tf_op jit(solution)/shard_map/ppermute | solution.py:684
  53.1 5.8 %collective-permute-start.6 = (bf16[160,128]{1,0:T(8,128)(2,1)S(1)}, bf16[160,128]{1,0:T(8,128)(2,1)S(1)}, u32[]{:S(2)}, u32[]{:S(2)}) collective-permute-start(bf16[160,128]{1,0:T(8,128)(2,1)S(1)} %pad_maximum_fusion.1), channel_id=1, source_target_pairs={{0,12},{1,13},{2,14},{3,15},{4,8},{5,9},{6,10},{7,11},{8,4},{9,5},... | collective-permute-start | bytes 122888 | tf_op jit(solution)/shard_map/ppermute | solution.py:684
  53.7 0.6 %copy-start.2 = (bf16[256,128]{1,0:T(8,128)(2,1)}, bf16[256,128]{1,0:T(8,128)(2,1)S(1)}, u32[]{:S(2)}) copy-start(bf16[256,128]{1,0:T(8,128)(2,1)S(1)} %collective-permute-done.7.second_hbm) | copy-start | bytes 196612
  59.0 1.4 %collective-permute-start.8 = (f32[256,128]{1,0:T(8,128)S(1)}, f32[256,128]{1,0:T(8,128)S(1)}, u32[]{:S(2)}, u32[]{:S(2)}) collective-permute-start(f32[256,128]{1,0:T(8,128)S(1)} %pad_maximum_fusion), channel_id=1, source_target_pairs={{0,1},{1,0},{2,3},{3,2},{4,5},{5,4},{6,7},{7,6},{8,9},{9,8},{10,11... | collective-permute-start | bytes 393224 | tf_op jit(solution)/shard_map/ppermute | solution.py:684
where the time goes:
time: 61.6 us; the launch traced here: 61.1 us
  Pallas kernels  31.1 us (50%)
  starting transfers between devices  16.6 us (27%)
  waiting for transfers between devices  10.4 us (17%)
  local copies, waits for them, and re-layouts  1.26 us (2%)
  other arithmetic  1.07 us (2%)
  between operations  0.81 us (1%)
    pallas_call x1, Pallas kernels, per_device(): pl.pallas_call(slope_kernel, out_shape=(jax.ShapeDtypeStruct((edge_count,...  11.6 us
    pallas_call x1, Pallas kernels, per_device(): pl.pallas_call(functools.partial(edge_kernel, coarse_scale), out_shape=(j...  10.5 us
    all_to_all x1, starting transfers between devices, per_device(): lax.all_to_all(sent, 'curve', split_axis=0, concat_axis=0, tiled=True)  8.25 us
    ppermute x5, starting transfers between devices, swapped(): return lax.ppermute(values, 'curve', [(i, i ^ hops) for i in range(peers)])  5.74 us
    pallas_call x1, Pallas kernels, per_device(): pl.pallas_call(functools.partial(coarse_kernel, peers), out_shape=jax.Sha...  4.88 us
    ppermute x5, waiting for transfers between devices, swapped(): return lax.ppermute(values, 'curve', [(i, i ^ hops) for i in range(peers)])  4.74 us
    all_to_all x1, waiting for transfers between devices, per_device(): lax.all_to_all(sent, 'curve', split_axis=0, concat_axis=0, tiled=True)  4.38 us
    pallas_call x1, Pallas kernels, per_device(): pl.pallas_call(fine_kernel, out_shape=jax.ShapeDtypeStruct((fine_count, L...  3.35 us
  transfers between devices with their start and end apart: 10, of which 5 were waited for; matrix products, arithmetic and copies ran while one was open for 0% of the time, Pallas kernels for 32%

commit v1 on v0

--- a/solution.py
+++ b/solution.py
@@ -12,6 +12,7 @@
 LANES = 128
 SPAN = 256
 EXTRA = 16
+WEIGHTS = EXTRA - 2
 TILE = 512
 GROUP = 4
 SENDERS = 3
@@ -114,6 +115,12 @@
     return both[:, 0:LANES] + both[:, LANES:]
 
 
+def term_sizes(peers):
+    chunk = min(WEIGHTS, SPAN // peers)
+    half = (SPAN - chunk * peers) // 2
+    return chunk, half, -(-(half + 1) // EXTRA) * EXTRA
+
+
 def fetch(sources, targets, arrivals):
     copies = [
         pltpu.make_async_copy(source, target, arrivals.at[i])
@@ -134,7 +141,9 @@
     w_out_ref,
     gain_ref,
     sent_ref,
+    rest_ref,
     table_ref,
+    terms,
     *held,
 ):
     *held, arrivals = held
@@ -144,8 +153,14 @@
         copy.wait()
     latent_ref, grad_ref, weights_ref, rows_ref, w_in_ref, w_out_ref, gain_ref = held
     count = latent_ref.shape[0]
-    chunk = SPAN // peers
-    capacity = sent_ref.shape[1] - EXTRA - max(EXTRA, chunk)
+    chunk, half_rest, rest_rows = term_sizes(peers)
+    capacity = sent_ref.shape[1] - EXTRA
+    per_step = 256 // LANES
+    steps = range(0, rows_ref.shape[0], per_step)
+    slots = []
+    for first in steps:
+        cols = index_columns(rows_ref, first, per_step)
+        slots.append((place_hot(cols), cols // SPAN))
     w_in, w_out, gain = w_in_ref[...], w_out_ref[...], gain_ref[...]
     latent = latent_ref[...]
     pre = dot(latent, w_in)
@@ -181,13 +196,16 @@
             table_ref[
                 half * LANES : (half + 1) * LANES, block * SPAN + LANES : (block + 1) * SPAN
             ] = square.T.astype(BF16)
-    gain_high, gain_low = two_parts(term_gain)
-    gain_rows = jnp.concatenate([gain_high.astype(F32), gain_low.astype(F32)], axis=0)
-    terms = jnp.concatenate([term_in, term_out], axis=0)
-    per_step = 256 // LANES
-    for first in range(0, rows_ref.shape[0], per_step):
-        cols = index_columns(rows_ref, first, per_step)
-        sent, weight = gather_rows(place_hot(cols), cols // SPAN, table_ref, SPAN)
+    terms[0:LANES, :] = term_in
+    terms[LANES:, :] = term_out
+    rest_ref[...] = jnp.zeros(rest_ref.shape, F32)
+    shared = chunk * peers
+    if half_rest:
+        rest_ref[0:half_rest, :] = terms[shared : shared + half_rest, :]
+        rest_ref[rest_rows : rest_rows + half_rest, :] = terms[shared + half_rest :, :]
+    rest_ref[half_rest : half_rest + 1, :] = term_gain
+    found = [gather_rows(hot, block, table_ref, SPAN) for hot, block in slots]
+    for first, (sent, weight) in zip(steps, found):
         for part in range(per_step * LANES // capacity):
             peer = first * LANES // capacity + part
             rows = slice(part * capacity, (part + 1) * capacity)
@@ -197,15 +215,12 @@
                 square = jnp.concatenate(
                     [square, jnp.zeros((LANES - capacity, LANES), F32)], axis=0
                 )
-            extra = jnp.concatenate(
-                [square.T[0:2], gain_rows, jnp.zeros((EXTRA - 4, LANES), F32)], axis=0
-            )
-            sent_ref[peer, capacity : capacity + EXTRA, :] = extra.astype(BF16)
             first_row = (peer % 2 * (peers // 2) + peer // 2) * chunk
-            share = terms[first_row : first_row + chunk]
-            if chunk < EXTRA:
-                share = jnp.concatenate([share, jnp.zeros((EXTRA - chunk, LANES), F32)], axis=0)
-            sent_ref[peer, capacity + EXTRA :, :] = share.astype(BF16)
+            extra = [terms[first_row : first_row + chunk, :]]
+            if chunk < WEIGHTS:
+                extra.append(jnp.zeros((WEIGHTS - chunk, LANES), F32))
+            extra.append(square.T[0:2])
+            sent_ref[peer, capacity:, :] = jnp.concatenate(extra, axis=0).astype(BF16)
 
 
 def order_edges(recv_ref, off_ref, ordered, stats_vmem, fine_count):
@@ -467,7 +482,6 @@
 
 
 def edge_kernel(
-    coarse_scale,
     stats,
     arrived_hbm,
     slot_hot_hbm,
@@ -479,12 +493,12 @@
     window_hbm,
     slope_sum_hbm,
     weight_hbm,
+    rest_hbm,
     grad_table,
     send_sum,
     first_ref,
     second_ref,
     keep_ref,
-    gain_ref,
     slot_table,
     grad_rows,
     arrived_ref,
@@ -497,6 +511,7 @@
     window,
     slope_sum,
     weight_ref,
+    rest_ref,
     arrivals,
 ):
     fine_count = grad_table.shape[0]
@@ -512,6 +527,7 @@
             window_hbm,
             slope_sum_hbm,
             weight_hbm,
+            rest_hbm,
         ),
         (
             arrived_ref,
@@ -524,31 +540,29 @@
             window,
             slope_sum,
             weight_ref,
+            rest_ref,
         ),
         arrivals,
     )
     send_sum[...] = jnp.zeros(send_sum.shape, F32)
     peers = arrived_ref.shape[0]
-    share = max(EXTRA, SPAN // peers)
-    capacity = arrived_ref.shape[1] - EXTRA - share
+    half = LANES + rest_ref.shape[0] // 2
+    capacity = arrived_ref.shape[1] - EXTRA
     per_block = SPAN // capacity
     for copy in copies[:3]:
         copy.wait()
-    coarse = jnp.zeros((share, LANES), F32)
-    gain = jnp.zeros((1, LANES), F32)
+    coarse = jnp.zeros((EXTRA, LANES), F32)
     for peer in range(peers):
         block, part = divmod(peer, per_block)
         rows = slice(part * capacity, (part + 1) * capacity)
         slot_table[rows, block * SPAN : block * SPAN + LANES] = arrived_ref[peer, 0:capacity, :]
-        extra = arrived_ref[peer, capacity : capacity + EXTRA, :].astype(F32)
+        extra = arrived_ref[peer, capacity:, :].astype(F32)
         square = jnp.concatenate([extra, jnp.zeros((LANES - EXTRA, LANES), F32)], axis=0).T
         slot_table[rows, block * SPAN + LANES : (block + 1) * SPAN] = square[0:capacity].astype(
             BF16
         )
-        gain += extra[2:3] + extra[3:4]
-        coarse += arrived_ref[peer, capacity + EXTRA :, :].astype(F32)
-    keep_ref[LANES:, :] = coarse
-    gain_ref[...] = gain * coarse_scale
+        coarse += extra
+    keep_ref[half:, :] = coarse
 
     found = []
     for first in range(0, slot_hot.shape[0], SPAN):
@@ -557,7 +571,8 @@
     for i, (grad, weight) in enumerate(found):
         first = i * SPAN
         for r in range(2):
-            rows = (grad * weight[:, r : r + 1]).astype(BF16).astype(F32)
+            factor = weight[:, WEIGHTS + r : WEIGHTS + r + 1]
+            rows = (grad * factor).astype(BF16).astype(F32)
             grad_rows[pl.ds(2 * first + r, SPAN, stride=2), :] = rows
     grad_table[...] = grad_rows[...].astype(BF16)
     for copy in copies[3:]:
@@ -599,7 +614,7 @@
     odd = lax.axis_index("curve") & 1
     to_prev = back(send_sum[0:HB, :], weight_send)
     to_next = back(send_sum[HB + fine_count :, :], weight_send)
-    first_ref[LANES:, :] = jnp.where(odd == 0, to_next, to_prev).astype(BF16)
+    first_ref[half:, :] = jnp.where(odd == 0, to_next, to_prev).astype(BF16)
     second_ref[...] = jnp.where(odd == 0, to_prev, to_next).astype(BF16)
     term_send = jnp.zeros((LANES, LANES), F32)
     term_recv = jnp.zeros((LANES, LANES), F32)
@@ -612,6 +627,9 @@
         term_recv += outer(window[moved, :], grad_rows[at, :] * slope_sum[at, :])
     keep_ref[0:LANES, :] = jnp.where(odd == 0, term_send, term_recv)
     first_ref[0:LANES, :] = jnp.where(odd == 0, term_recv, term_send).astype(BF16)
+    rest_first, rest_second = rest_ref[0 : half - LANES, :], rest_ref[half - LANES :, :]
+    keep_ref[LANES:half, :] = jnp.where(odd == 0, rest_first, rest_second)
+    first_ref[LANES:half, :] = jnp.where(odd == 0, rest_second, rest_first).astype(BF16)
 
 
 def fine_kernel(
@@ -638,7 +656,8 @@
     ):
         copy.wait()
     odd = lax.axis_index("curve") & 1
-    one, two = first_ref[LANES:, :].astype(F32), second_ref[...].astype(F32)
+    half = first_ref.shape[0] - HB
+    one, two = first_ref[half:, :].astype(F32), second_ref[...].astype(F32)
     from_next, from_prev = jnp.where(odd == 0, one, two), jnp.where(odd == 0, two, one)
     for first in range(0, fine_count, SPAN):
         at = slice(first, first + SPAN)
@@ -657,15 +676,39 @@
 
 
 def last_kernel(
-    edge_scale, coarse_scale, own_ref, coarse_ref, there_ref, edge_ref, in_ref, out_ref
+    edge_scale,
+    coarse_scale,
+    peers,
+    own_ref,
+    coarse_ref,
+    there_ref,
+    edge_ref,
+    in_ref,
+    out_ref,
+    gain_ref,
+    terms,
 ):
+    chunk, half_rest, _ = term_sizes(peers)
+    half = own_ref.shape[0]
     odd = lax.axis_index("curve") & 1
     own, coarse = own_ref[...], coarse_ref[...].astype(F32)
-    other, other_coarse = there_ref[0:LANES, :], there_ref[LANES:, :]
-    edge_ref[0:LANES, :] = jnp.where(odd == 0, own, other) * edge_scale
-    edge_ref[LANES:, :] = jnp.where(odd == 0, other, own) * edge_scale
-    in_ref[...] = jnp.where(odd == 0, coarse, other_coarse) * coarse_scale
-    out_ref[...] = jnp.where(odd == 0, other_coarse, coarse) * coarse_scale
+    other, other_coarse = there_ref[0:half, :], there_ref[half:, :]
+    halves = (jnp.where(odd == 0, own, other), jnp.where(odd == 0, other, own))
+    shares = (
+        jnp.where(odd == 0, coarse, other_coarse),
+        jnp.where(odd == 0, other_coarse, coarse),
+    )
+    for core in range(2):
+        edge_ref[core * LANES : (core + 1) * LANES, :] = halves[core][0:LANES] * edge_scale
+        for i in range(peers // 2):
+            at = (core * (peers // 2) + i) * chunk
+            terms[at : at + chunk, :] = shares[core][i * EXTRA : i * EXTRA + chunk]
+        if half_rest:
+            at = chunk * peers + core * half_rest
+            terms[at : at + half_rest, :] = halves[core][LANES : LANES + half_rest]
+    in_ref[...] = terms[0:LANES, :] * coarse_scale
+    out_ref[...] = terms[LANES:, :] * coarse_scale
+    gain_ref[...] = halves[0][LANES + half_rest : LANES + half_rest + 1] * coarse_scale
 
 
 def pair_exchange(first, second, peers):
@@ -726,9 +769,9 @@
     fine_count = fine_latent.shape[0]
     edge_count = edge_receivers.shape[0]
     capacity = send_rows.shape[0] // peers
-    chunk = SPAN // peers
-    share = max(EXTRA, chunk)
-    payload = capacity + EXTRA + share
+    rest_rows = term_sizes(peers)[2]
+    half = LANES + rest_rows
+    payload = capacity + EXTRA
     edge_rows = edge_count // LANES
     window_count = fine_count + 2 * HB
     params = pltpu.CompilerParams(vmem_limit_bytes=64 * 1024 * 1024 - 256 * 1024)
@@ -740,12 +783,16 @@
     head, end = fine_latent[:HB], fine_latent[fine_count - HB :]
     halos = pair_exchange(jnp.where(even, end, head), jnp.where(even, head, end), peers)
 
-    sent = pl.pallas_call(
+    sent, rest = pl.pallas_call(
         functools.partial(coarse_kernel, peers),
-        out_shape=jax.ShapeDtypeStruct((peers, payload, LANES), BF16),
+        out_shape=(
+            jax.ShapeDtypeStruct((peers, payload, LANES), BF16),
+            jax.ShapeDtypeStruct((2 * rest_rows, LANES), F32),
+        ),
         in_specs=[anywhere] * 7,
         scratch_shapes=[
             pltpu.VMEM((SPAN, coarse_count), BF16),
+            pltpu.VMEM((2 * LANES, LANES), F32),
             pltpu.VMEM((coarse_count, LANES), BF16),
             pltpu.VMEM((coarse_count, LANES), BF16),
             pltpu.VMEM((2, coarse_count), BF16),
@@ -820,17 +867,16 @@
 
     coarse_scale = 1.0 / math.sqrt(coarse_count * peers)
     edge_scale = 1.0 / math.sqrt(edge_count * peers)
-    grad_rows, send_sum, first, second, keep, term_gain = pl.pallas_call(
-        functools.partial(edge_kernel, coarse_scale),
+    grad_rows, send_sum, first, second, keep = pl.pallas_call(
+        edge_kernel,
         out_shape=(
             jax.ShapeDtypeStruct((fine_count, LANES), BF16),
             jax.ShapeDtypeStruct((window_count, LANES), F32),
-            pltpu.VMEM((LANES + HB, LANES), BF16),
+            pltpu.VMEM((half + HB, LANES), BF16),
             pltpu.VMEM((HB, LANES), BF16),
-            pltpu.VMEM((LANES + share, LANES), F32),
-            jax.ShapeDtypeStruct((1, LANES), F32),
-        ),
-        in_specs=[scalar] + [anywhere] * 10,
+            pltpu.VMEM((half + EXTRA, LANES), F32),
+        ),
+        in_specs=[scalar] + [anywhere] * 11,
         scratch_shapes=[
             pltpu.VMEM((SPAN, peers * capacity), BF16),
             pltpu.VMEM((fine_count, LANES), F32),
@@ -844,7 +890,8 @@
             pltpu.VMEM((window_count, LANES), BF16),
             pltpu.VMEM((fine_count, LANES), F32),
             pltpu.VMEM((2 * LANES, LANES), BF16),
-            pltpu.SemaphoreType.DMA((10,)),
+            pltpu.VMEM((2 * rest_rows, LANES), F32),
+            pltpu.SemaphoreType.DMA((11,)),
         ],
         compiler_params=roomy,
         cost_estimate=pl.CostEstimate(
@@ -863,9 +910,10 @@
         window,
         slope_sum,
         edge_weight,
+        rest,
     )
     one, two = pair_exchange(first, second, peers)
-    sent = keep[: LANES + chunk] + jnp.pad(one[:LANES].astype(F32), ((0, chunk), (0, 0)))
+    sent = keep + jnp.pad(one[:half].astype(F32), ((0, EXTRA), (0, 0)))
     sent = sent.astype(BF16)
     grad_fine = pl.pallas_call(
         fine_kernel,
@@ -876,7 +924,7 @@
             pltpu.VMEM((window_count, LANES), F32),
             pltpu.VMEM((fine_count, LANES), F32),
             pltpu.VMEM((2 * LANES, LANES), BF16),
-            pltpu.VMEM((LANES + HB, LANES), BF16),
+            pltpu.VMEM((half + HB, LANES), BF16),
             pltpu.VMEM((HB, LANES), BF16),
             pltpu.SemaphoreType.DMA((6,)),
         ],
@@ -886,15 +934,17 @@
         ),
         name="fine_sums",
     )(grad_rows, send_sum, slope_sum, edge_weight, one, two)
-    own, coarse, grad_fine = reduced(sent, LANES, device, peers, grad_fine)
+    own, coarse, grad_fine = reduced(sent, half, device, peers, grad_fine)
     there = swapped(jnp.concatenate([own, coarse.astype(F32)], axis=0), 1, peers)
-    edge_terms, term_in, term_out = pl.pallas_call(
-        functools.partial(last_kernel, edge_scale, coarse_scale),
+    edge_terms, term_in, term_out, term_gain = pl.pallas_call(
+        functools.partial(last_kernel, edge_scale, coarse_scale, peers),
         out_shape=(
             jax.ShapeDtypeStruct((2 * LANES, LANES), F32),
             jax.ShapeDtypeStruct((LANES, LANES), F32),
             jax.ShapeDtypeStruct((LANES, LANES), F32),
-        ),
+            jax.ShapeDtypeStruct((1, LANES), F32),
+        ),
+        scratch_shapes=[pltpu.VMEM((2 * LANES, LANES), F32)],
         compiler_params=pltpu.CompilerParams(vmem_limit_bytes=4 * 1024 * 1024),
         name="last_terms",
     )(own, coarse, there)

time: 61.6 us -> 60.1 us (0.976)
  waiting for transfers between devices: 10.4 us -> 9.39 us
    all_to_all x1, waiting for transfers between devices: 4.38 us -> 3.34 us  [per_device(): lax.all_to_all(sent, 'curve', split_axis=0, concat_axis=0, tiled=True)]
  transfers between devices with their start and end apart: 10 -> 10, of which waited for: 5 -> 5; matrix products, arithmetic and copies ran while one was open for 0% -> 0% of each run, Pallas kernels for 32% -> 33%
where the time goes in v1:
time: 60.1 us; the launch traced here: 59.6 us
  Pallas kernels  30.7 us (51%)
  starting transfers between devices  16.3 us (27%)
  waiting for transfers between devices  9.39 us (16%)
  local copies, waits for them, and re-layouts  1.26 us (2%)
  other arithmetic  1.08 us (2%)
  between operations  0.82 us (1%)
    pallas_call x1, Pallas kernels, per_device(): pl.pallas_call(slope_kernel, out_shape=(jax.ShapeDtypeStruct((edge_count,...  11.6 us
    pallas_call x1, Pallas kernels, per_device(): pl.pallas_call(edge_kernel, out_shape=(jax.ShapeDtypeStruct((fine_count,...  10.3 us
    all_to_all x1, starting transfers between devices, per_device(): lax.all_to_all(sent, 'curve', split_axis=0, concat_axis=0, tiled=True)  8.27 us
    ppermute x5, starting transfers between devices, swapped(): return lax.ppermute(values, 'curve', [(i, i ^ hops) for i in range(peers)])  5.57 us
    ppermute x5, waiting for transfers between devices, swapped(): return lax.ppermute(values, 'curve', [(i, i ^ hops) for i in range(peers)])  4.75 us
    pallas_call x1, Pallas kernels, per_device(): pl.pallas_call(functools.partial(coarse_kernel, peers), out_shape=(jax.Sh...  4.74 us
    pallas_call x1, Pallas kernels, per_device(): pl.pallas_call(fine_kernel, out_shape=jax.ShapeDtypeStruct((fine_count, L...  3.36 us
    all_to_all x1, waiting for transfers between devices, per_device(): lax.all_to_all(sent, 'curve', split_axis=0, concat_axis=0, tiled=True)  3.34 us
  transfers between devices with their start and end apart: 10, of which 5 were waited for; matrix products, arithmetic and copies ran while one was open for 0% of the time, Pallas kernels for 33%

profile of v1, /device:TPU:0, one launch (start us, length us, event | category | flops | bytes accessed | tf_op | source)
XLA Modules:
  0.0 59.6 jit_solution(683421006866722421)
XLA Ops:
  0.6 0.9 %broadcast_select_fusion = (bf16[256,128]{1,0:T(8,128)(2,1)S(1)}, bf16[256,128]{1,0:T(8,128)(2,1)S(1)}) fusion(pred[]{:T(512)S(6)} %eq.3, bf16[2048,128]{1,0:T(8,128)(2,1)} %fine_hbm.1), kind=kLoop, calls=%fused_computation.4 | loop fusion | flops 65536 | bytes 262145 | tf_op jit(solution)/shard_map/jit(_where)/select_n | solution.py:784
  1.5 0.5 collective-permute-start
  2.0 1.3 %collective-permute-start.1 = (bf16[256,128]{1,0:T(8,128)(2,1)S(1)}, bf16[256,128]{1,0:T(8,128)(2,1)}, u32[]{:S(2)}, u32[]{:S(2)}) collective-permute-start(bf16[256,128]{1,0:T(8,128)(2,1)S(1)} %get-tuple-element.57), channel_id=1, source_target_pairs={{1,2},{2,1},{3,4},{4,3},{5,6},{6,5},{7,8},{8,7},{9,10},{10,9},{11,... | collective-permute-start | bytes 196616 | tf_op jit(solution)/shard_map/ppermute | solution.py:717
  3.3 4.7 %coarse_block.1 = (bf16[16,144,128]{2,1,0:T(8,128)(2,1)}, f32[64,128]{1,0:T(8,128)}) custom-call(bf16[1024,128]{1,0:T(8,128)(2,1)} %latent_ref.1, bf16[1024,128]{1,0:T(8,128)(2,1)} %grad_ref.1, bf16[2,1024]{1,0:T(2,128)(2,1)} %weights_ref.1, s32[16,128]{1,0:T(8,128)} %bitcast.8, bf16[128,128]{1,0:T(8,128)(2,1)} %w_in_ref.1, bf16[128,128]{1,0:T(8,128)(2,1)} %w_out_ref.1, ...), custom_call_target="tpu_custom_call" | custom-call | flops 2000000000 | bytes 2000000 | tf_op jit(solution)/shard_map/coarse_block/pallas_call | solution.py:786
  8.1 8.3 %all-to-all-start = ((bf16[16,144,128]{2,1,0:T(8,128)(2,1)}), bf16[16,144,128]{2,1,0:T(8,128)(2,1)}, u32[]{:S(2)}, u32[]{:S(2)}) async-start(bf16[16,144,128]{2,1,0:T(8,128)(2,1)} %get-tuple-element.31), calls=%async_computation | async-start | bytes 1179648 | tf_op jit(solution)/shard_map/all_to_all | solution.py:819
  16.4 0.6 %copy-done.3 = bf16[256,128]{1,0:T(8,128)(2,1)} copy-done((bf16[256,128]{1,0:T(8,128)(2,1)}, bf16[256,128]{1,0:T(8,128)(2,1)S(1)}, u32[]{:S(2)}) %copy-start.3) | copy-done | bytes 65560
  17.0 11.6 %edge_slope.1 = (f32[6144,128]{1,0:T(8,128)}, bf16[6144,256]{1,0:T(8,128)(2,1)}, bf16[6144,128]{1,0:T(8,128)(2,1)}, bf16[2560,128]{1,0:T(8,128)(2,1)}, f32[2048,...) custom-call(s32[48,128]{1,0:T(8,128)} %bitcast.6, ...), custom_call_target="tpu_custom_call" | custom-call | flops 16000000000 | bytes 5000000 | tf_op jit(solution)/shard_map/edge_slope/pallas_call | solution.py:823
  28.6 3.3 %all-to-all-done.arrived_hbm = bf16[16,144,128]{2,1,0:T(8,128)(2,1)} async-done(((bf16[16,144,128]{2,1,0:T(8,128)(2,1)}), bf16[16,144,128]{2,1,0:T(8,128)(2,1)}, u32[]{:S(2)}, u32[]{:S(2)}) %all-to-all-start) | async-done | bytes 589856 | tf_op jit(solution)/shard_map/all_to_all | solution.py:819
  31.9 10.3 %edge_back.1 = (bf16[2048,128]{1,0:T(8,128)(2,1)}, f32[2560,128]{1,0:T(8,128)}, bf16[416,128]{1,0:T(8,128)(2,1)S(1)}, bf16[256,128]{1,0:T(8,128)(2,1)S(1)}, f32[176,128]{1,0:T(8,128)S(1)}) custom-call(s32[48,128]{1,0:T(8,128)} %get-tuple-element.30.stats, bf16[16,144,128]{2,1,0:T(8,128)(2,1)} %all-to-all-done.arrived_hbm, ...), custom_call_target="tpu_custom_call" | custom-call | flops 24000000000 | bytes 8000000 | tf_op jit(solution)/shard_map/edge_back/pallas_call | solution.py:870
  42.2 0.1 collective-permute-start.2
  42.3 1.3 %collective-permute-done.2.first_hbm = bf16[416,128]{1,0:T(8,128)(2,1)S(1)} collective-permute-done((bf16[416,128]{1,0:T(8,128)(2,1)S(1)}, bf16[416,128]{1,0:T(8,128)(2,1)S(1)}, u32[]{:S(2)}, u32[]{:S(2)}) %collective-permute-start.2) | collective-permute-done | bytes 106528 | tf_op jit(solution)/shard_map/ppermute | solution.py:717
  43.6 0.1 add_convert_fusion
  43.7 1.0 %collective-permute-start.3 = (bf16[176,128]{1,0:T(8,128)(2,1)S(1)}, bf16[176,128]{1,0:T(8,128)(2,1)S(1)}, u32[]{:S(2)}, u32[]{:S(2)}) collective-permute-start(bf16[176,128]{1,0:T(8,128)(2,1)S(1)} %add_convert_fusion), channel_id=1, source_target_pairs={{0,2},{1,3},{2,0},{3,1},{4,6},{5,7},{6,4},{7,5},{8,10},{9,11},{10,... | collective-permute-start | bytes 135176 | tf_op jit(solution)/shard_map/ppermute | solution.py:727
  44.7 0.7 %collective-permute-start.7 = (bf16[256,128]{1,0:T(8,128)(2,1)S(1)}, bf16[256,128]{1,0:T(8,128)(2,1)S(1)}, u32[]{:S(2)}, u32[]{:S(2)}) collective-permute-start(bf16[256,128]{1,0:T(8,128)(2,1)S(1)} %get-tuple-element.45), channel_id=1, source_target_pairs={{1,2},{2,1},{3,4},{4,3},{5,6},{6,5},{7,8},{8,7},{9,10},{10,9},{11,... | collective-permute-start | bytes 196616 | tf_op jit(solution)/shard_map/ppermute | solution.py:717
  45.4 2.4 %collective-permute-done.3 = bf16[176,128]{1,0:T(8,128)(2,1)S(1)} collective-permute-done((bf16[176,128]{1,0:T(8,128)(2,1)S(1)}, bf16[176,128]{1,0:T(8,128)(2,1)S(1)}, u32[]{:S(2)}, u32[]{:S(2)}) %collective-permute-start.3) | collective-permute-done | bytes 45088 | tf_op jit(solution)/shard_map/ppermute | solution.py:727
  47.9 1.8 %collective-permute-start.4 = (bf16[192,128]{1,0:T(8,128)(2,1)S(1)}, bf16[192,128]{1,0:T(8,128)(2,1)S(1)}, u32[]{:S(2)}, u32[]{:S(2)}) collective-permute-start(bf16[192,128]{1,0:T(8,128)(2,1)S(1)} %pad_maximum_fusion.1), channel_id=1, source_target_pairs={{0,4},{1,5},{2,6},{3,7},{4,0},{5,1},{6,2},{7,3},{8,12},{9,13},{10,... | collective-permute-start | bytes 147464 | tf_op jit(solution)/shard_map/ppermute | solution.py:727
  49.6 1.7 %collective-permute-start.5 = (bf16[192,128]{1,0:T(8,128)(2,1)S(1)}, bf16[192,128]{1,0:T(8,128)(2,1)S(1)}, u32[]{:S(2)}, u32[]{:S(2)}) collective-permute-start(bf16[192,128]{1,0:T(8,128)(2,1)S(1)} %pad_maximum_fusion.1), channel_id=1, source_target_pairs={{0,8},{1,9},{2,10},{3,11},{4,12},{5,13},{6,14},{7,15},{8,0},{9,1},... | collective-permute-start | bytes 147464 | tf_op jit(solution)/shard_map/ppermute | solution.py:727
  51.3 1.0 %collective-permute-start.6 = (bf16[192,128]{1,0:T(8,128)(2,1)S(1)}, bf16[192,128]{1,0:T(8,128)(2,1)S(1)}, u32[]{:S(2)}, u32[]{:S(2)}) collective-permute-start(bf16[192,128]{1,0:T(8,128)(2,1)S(1)} %pad_maximum_fusion.1), channel_id=1, source_target_pairs={{0,12},{1,13},{2,14},{3,15},{4,8},{5,9},{6,10},{7,11},{8,4},{9,5},... | collective-permute-start | bytes 147464 | tf_op jit(solution)/shard_map/ppermute | solution.py:727
  52.3 0.6 %copy-done.2 = bf16[256,128]{1,0:T(8,128)(2,1)} copy-done((bf16[256,128]{1,0:T(8,128)(2,1)}, bf16[256,128]{1,0:T(8,128)(2,1)S(1)}, u32[]{:S(2)}) %copy-start.2) | copy-done | bytes 65560
  52.9 3.4 %fine_sums.1 = bf16[2048,128]{1,0:T(8,128)(2,1)} custom-call(bf16[2048,128]{1,0:T(8,128)(2,1)} %get-tuple-element.43.grad_hbm, f32[2560,128]{1,0:T(8,128)} %get-tuple-element.44.send_sum_hbm, f32[2048,128]{1,0:T(8,128)} %get-tuple-element.39.slope_sum_hbm, bf16[256,128]{1,0:T(8,128)(2,1)} %weight_hbm.5, bf16[416,128]{1,0:T(8,128)(2,1)} %copy-done, ...), custom_call_target="tpu_custom_call" | custom-call | flops 1000000000 | bytes 4000000 | tf_op jit(solution)/shard_map/fine_sums/pallas_call | solution.py:918
  56.3 1.0 %collective-permute-done.6 = bf16[192,128]{1,0:T(8,128)(2,1)S(1)} collective-permute-done((bf16[192,128]{1,0:T(8,128)(2,1)S(1)}, bf16[192,128]{1,0:T(8,128)(2,1)S(1)}, u32[]{:S(2)}, u32[]{:S(2)}) %collective-permute-start.6) | collective-permute-done | bytes 49184 | tf_op jit(solution)/shard_map/ppermute | solution.py:727
  57.4 0.1 collective-permute-start.8
  57.5 1.4 %collective-permute-done.8.there_ref = f32[288,128]{1,0:T(8,128)S(1)} collective-permute-done((f32[288,128]{1,0:T(8,128)S(1)}, f32[288,128]{1,0:T(8,128)S(1)}, u32[]{:S(2)}, u32[]{:S(2)}) %collective-permute-start.8) | collective-permute-done | bytes 147488 | tf_op jit(solution)/shard_map/ppermute | solution.py:727
  58.9 0.7 %last_terms.1 = (f32[256,128]{1,0:T(8,128)}, f32[128,128]{1,0:T(8,128)}, f32[128,128]{1,0:T(8,128)}, f32[1,128]{1,0:T(1,128)}) custom-call(f32[160,128]{1,0:T(8,128)S(1)} %add_add_fusion.own_ref, bf16[128,128]{1,0:T(8,128)(2,1)S(1)} %get-tuple-element.56.coarse_ref, f32[288,128]{1,0:T(8,128)S(1)} %collective-permute-done.8.there_ref), custom_call_target="tpu_custom_call" | custom-call | tf_op jit(solution)/shard_map/last_terms/pallas_call | solution.py:939
  (24 shorter events, 0.1 us)
Async XLA Ops:
  1.5 14.8 %collective-permute-start = (bf16[256,128]{1,0:T(8,128)(2,1)S(1)}, bf16[256,128]{1,0:T(8,128)(2,1)S(1)}, u32[]{:S(2)}, u32[]{:S(2)}) collective-permute-start(bf16[256,128]{1,0:T(8,128)(2,1)S(1)} %get-tuple-element.58), channel_id=1, source_target_pairs={{0,1},{1,0},{2,3},{3,2},{4,5},{5,4},{6,7},{7,6},{8,9},{9,8},{10,11... | collective-permute-start | bytes 196616 | tf_op jit(solution)/shard_map/ppermute | solution.py:717
  2.0 14.3 %collective-permute-start.1 = (bf16[256,128]{1,0:T(8,128)(2,1)S(1)}, bf16[256,128]{1,0:T(8,128)(2,1)}, u32[]{:S(2)}, u32[]{:S(2)}) collective-permute-start(bf16[256,128]{1,0:T(8,128)(2,1)S(1)} %get-tuple-element.57), channel_id=1, source_target_pairs={{1,2},{2,1},{3,4},{4,3},{5,6},{6,5},{7,8},{8,7},{9,10},{10,9},{11,... | collective-permute-start | bytes 196616 | tf_op jit(solution)/shard_map/ppermute | solution.py:717
  8.1 23.9 %all-to-all-start = ((bf16[16,144,128]{2,1,0:T(8,128)(2,1)}), bf16[16,144,128]{2,1,0:T(8,128)(2,1)}, u32[]{:S(2)}, u32[]{:S(2)}) async-start(bf16[16,144,128]{2,1,0:T(8,128)(2,1)} %get-tuple-element.31), calls=%async_computation | async-start | bytes 1179648 | tf_op jit(solution)/shard_map/all_to_all | solution.py:819
  16.4 0.6 %copy-start.3 = (bf16[256,128]{1,0:T(8,128)(2,1)}, bf16[256,128]{1,0:T(8,128)(2,1)S(1)}, u32[]{:S(2)}) copy-start(bf16[256,128]{1,0:T(8,128)(2,1)S(1)} %collective-permute-done.first_hbm) | copy-start | bytes 196612
  31.9 11.7 %copy-start.1 = (pred[176]{0:T(512)(128)(4,1)S(1)}, pred[176]{0:T(512)(128)(4,1)}, u32[]{:S(2)}) copy-start(pred[176]{0:T(512)(128)(4,1)} %constant.14.clone.1) | copy-start | bytes 532
  42.2 1.4 %collective-permute-start.2 = (bf16[416,128]{1,0:T(8,128)(2,1)S(1)}, bf16[416,128]{1,0:T(8,128)(2,1)S(1)}, u32[]{:S(2)}, u32[]{:S(2)}) collective-permute-start(bf16[416,128]{1,0:T(8,128)(2,1)S(1)} %get-tuple-element.42), channel_id=1, source_target_pairs={{0,1},{1,0},{2,3},{3,2},{4,5},{5,4},{6,7},{7,6},{8,9},{9,8},{10,11... | collective-permute-start | bytes 319496 | tf_op jit(solution)/shard_map/ppermute | solution.py:717
  43.6 8.7 %copy-start = (bf16[416,128]{1,0:T(8,128)(2,1)}, bf16[416,128]{1,0:T(8,128)(2,1)S(1)}, u32[]{:S(2)}) copy-start(bf16[416,128]{1,0:T(8,128)(2,1)S(1)} %collective-permute-done.2.first_hbm) | copy-start | bytes 319492
  43.7 4.1 %collective-permute-start.3 = (bf16[176,128]{1,0:T(8,128)(2,1)S(1)}, bf16[176,128]{1,0:T(8,128)(2,1)S(1)}, u32[]{:S(2)}, u32[]{:S(2)}) collective-permute-start(bf16[176,128]{1,0:T(8,128)(2,1)S(1)} %add_convert_fusion), channel_id=1, source_target_pairs={{0,2},{1,3},{2,0},{3,1},{4,6},{5,7},{6,4},{7,5},{8,10},{9,11},{10,... | collective-permute-start | bytes 135176 | tf_op jit(solution)/shard_map/ppermute | solution.py:727
  44.7 7.6 %collective-permute-start.7 = (bf16[256,128]{1,0:T(8,128)(2,1)S(1)}, bf16[256,128]{1,0:T(8,128)(2,1)S(1)}, u32[]{:S(2)}, u32[]{:S(2)}) collective-permute-start(bf16[256,128]{1,0:T(8,128)(2,1)S(1)} %get-tuple-element.45), channel_id=1, source_target_pairs={{1,2},{2,1},{3,4},{4,3},{5,6},{6,5},{7,8},{8,7},{9,10},{10,9},{11,... | collective-permute-start | bytes 196616 | tf_op jit(solution)/shard_map/ppermute | solution.py:717
  47.9 8.5 %collective-permute-start.4 = (bf16[192,128]{1,0:T(8,128)(2,1)S(1)}, bf16[192,128]{1,0:T(8,128)(2,1)S(1)}, u32[]{:S(2)}, u32[]{:S(2)}) collective-permute-start(bf16[192,128]{1,0:T(8,128)(2,1)S(1)} %pad_maximum_fusion.1), channel_id=1, source_target_pairs={{0,4},{1,5},{2,6},{3,7},{4,0},{5,1},{6,2},{7,3},{8,12},{9,13},{10,... | collective-permute-start | bytes 147464 | tf_op jit(solution)/shard_map/ppermute | solution.py:727
  49.6 6.7 %collective-permute-start.5 = (bf16[192,128]{1,0:T(8,128)(2,1)S(1)}, bf16[192,128]{1,0:T(8,128)(2,1)S(1)}, u32[]{:S(2)}, u32[]{:S(2)}) collective-permute-start(bf16[192,128]{1,0:T(8,128)(2,1)S(1)} %pad_maximum_fusion.1), channel_id=1, source_target_pairs={{0,8},{1,9},{2,10},{3,11},{4,12},{5,13},{6,14},{7,15},{8,0},{9,1},... | collective-permute-start | bytes 147464 | tf_op jit(solution)/shard_map/ppermute | solution.py:727
  51.3 6.0 %collective-permute-start.6 = (bf16[192,128]{1,0:T(8,128)(2,1)S(1)}, bf16[192,128]{1,0:T(8,128)(2,1)S(1)}, u32[]{:S(2)}, u32[]{:S(2)}) collective-permute-start(bf16[192,128]{1,0:T(8,128)(2,1)S(1)} %pad_maximum_fusion.1), channel_id=1, source_target_pairs={{0,12},{1,13},{2,14},{3,15},{4,8},{5,9},{6,10},{7,11},{8,4},{9,5},... | collective-permute-start | bytes 147464 | tf_op jit(solution)/shard_map/ppermute | solution.py:727
  52.3 0.6 %copy-start.2 = (bf16[256,128]{1,0:T(8,128)(2,1)}, bf16[256,128]{1,0:T(8,128)(2,1)S(1)}, u32[]{:S(2)}) copy-start(bf16[256,128]{1,0:T(8,128)(2,1)S(1)} %collective-permute-done.7.second_hbm) | copy-start | bytes 196612
  57.4 1.4 %collective-permute-start.8 = (f32[288,128]{1,0:T(8,128)S(1)}, f32[288,128]{1,0:T(8,128)S(1)}, u32[]{:S(2)}, u32[]{:S(2)}) collective-permute-start(f32[288,128]{1,0:T(8,128)S(1)} %pad_maximum_fusion), channel_id=1, source_target_pairs={{0,1},{1,0},{2,3},{3,2},{4,5},{5,4},{6,7},{7,6},{8,9},{9,8},{10,11... | collective-permute-start | bytes 442376 | tf_op jit(solution)/shard_map/ppermute | solution.py:727

commit v2 on v1

--- a/solution.py
+++ b/solution.py
@@ -105,8 +105,8 @@
 
 
 def back(values, weight):
-    high, low = two_parts(values)
-    return dot(high, weight, NT) + dot(low, weight, NT)
+    both = jnp.concatenate(two_parts(values), axis=1)
+    return dot(both, jnp.concatenate([weight, weight], axis=1), NT)
 
 
 def outer(rows, values):
@@ -928,7 +928,7 @@
             pltpu.VMEM((HB, LANES), BF16),
             pltpu.SemaphoreType.DMA((6,)),
         ],
-        compiler_params=pltpu.CompilerParams(vmem_limit_bytes=64 * 1024 * 1024 - 640 * 1024),
+        compiler_params=pltpu.CompilerParams(vmem_limit_bytes=64 * 1024 * 1024 - 1536 * 1024),
         cost_estimate=pl.CostEstimate(
             flops=1_000_000_000, bytes_accessed=4_000_000, transcendentals=0
         ),

time: 60.1 us -> 60 us (level)
  no operation moved by 1% of the time
where the time goes in v2:
time: 60 us; the launch traced here: 59.6 us
  Pallas kernels  30.7 us (51%)
  starting transfers between devices  16.4 us (27%)
  waiting for transfers between devices  9.4 us (16%)
  local copies, waits for them, and re-layouts  1.26 us (2%)
  other arithmetic  1.08 us (2%)
  between operations  0.81 us (1%)
    pallas_call x1, Pallas kernels, per_device(): pl.pallas_call(slope_kernel, out_shape=(jax.ShapeDtypeStruct((edge_count,...  11.6 us
    pallas_call x1, Pallas kernels, per_device(): pl.pallas_call(edge_kernel, out_shape=(jax.ShapeDtypeStruct((fine_count,...  10.2 us
    all_to_all x1, starting transfers between devices, per_device(): lax.all_to_all(sent, 'curve', split_axis=0, concat_axis=0, tiled=True)  8.27 us
    ppermute x5, starting transfers between devices, swapped(): return lax.ppermute(values, 'curve', [(i, i ^ hops) for i in range(peers)])  5.58 us
    ppermute x5, waiting for transfers between devices, swapped(): return lax.ppermute(values, 'curve', [(i, i ^ hops) for i in range(peers)])  4.79 us
    pallas_call x1, Pallas kernels, per_device(): pl.pallas_call(functools.partial(coarse_kernel, peers), out_shape=(jax.Sh...  4.74 us
    pallas_call x1, Pallas kernels, per_device(): pl.pallas_call(fine_kernel, out_shape=jax.ShapeDtypeStruct((fine_count, L...  3.35 us
    all_to_all x1, waiting for transfers between devices, per_device(): lax.all_to_all(sent, 'curve', split_axis=0, concat_axis=0, tiled=True)  3.34 us
  transfers between devices with their start and end apart: 10, of which 5 were waited for; matrix products, arithmetic and copies ran while one was open for 0% of the time, Pallas kernels for 33%

profile of v2, /device:TPU:0, one launch (start us, length us, event | category | flops | bytes accessed | tf_op | source)
XLA Modules:
  0.0 59.6 jit_solution(6956877133132365831)
XLA Ops:
  0.6 0.9 %broadcast_select_fusion = (bf16[256,128]{1,0:T(8,128)(2,1)S(1)}, bf16[256,128]{1,0:T(8,128)(2,1)S(1)}) fusion(pred[]{:T(512)S(6)} %eq.3, bf16[2048,128]{1,0:T(8,128)(2,1)} %fine_hbm.1), kind=kLoop, calls=%fused_computation.4 | loop fusion | flops 65536 | bytes 262145 | tf_op jit(solution)/shard_map/jit(_where)/select_n | solution.py:784
  1.5 0.5 collective-permute-start
  2.0 1.3 %collective-permute-start.1 = (bf16[256,128]{1,0:T(8,128)(2,1)S(1)}, bf16[256,128]{1,0:T(8,128)(2,1)}, u32[]{:S(2)}, u32[]{:S(2)}) collective-permute-start(bf16[256,128]{1,0:T(8,128)(2,1)S(1)} %get-tuple-element.57), channel_id=1, source_target_pairs={{1,2},{2,1},{3,4},{4,3},{5,6},{6,5},{7,8},{8,7},{9,10},{10,9},{11,... | collective-permute-start | bytes 196616 | tf_op jit(solution)/shard_map/ppermute | solution.py:717
  3.3 4.7 %coarse_block.1 = (bf16[16,144,128]{2,1,0:T(8,128)(2,1)}, f32[64,128]{1,0:T(8,128)}) custom-call(bf16[1024,128]{1,0:T(8,128)(2,1)} %latent_ref.1, bf16[1024,128]{1,0:T(8,128)(2,1)} %grad_ref.1, bf16[2,1024]{1,0:T(2,128)(2,1)} %weights_ref.1, s32[16,128]{1,0:T(8,128)} %bitcast.8, bf16[128,128]{1,0:T(8,128)(2,1)} %w_in_ref.1, bf16[128,128]{1,0:T(8,128)(2,1)} %w_out_ref.1, ...), custom_call_target="tpu_custom_call" | custom-call | flops 2000000000 | bytes 2000000 | tf_op jit(solution)/shard_map/coarse_block/pallas_call | solution.py:786
  8.1 8.3 %all-to-all-start = ((bf16[16,144,128]{2,1,0:T(8,128)(2,1)}), bf16[16,144,128]{2,1,0:T(8,128)(2,1)}, u32[]{:S(2)}, u32[]{:S(2)}) async-start(bf16[16,144,128]{2,1,0:T(8,128)(2,1)} %get-tuple-element.31), calls=%async_computation | async-start | bytes 1179648 | tf_op jit(solution)/shard_map/all_to_all | solution.py:819
  16.4 0.6 %copy-done.3 = bf16[256,128]{1,0:T(8,128)(2,1)} copy-done((bf16[256,128]{1,0:T(8,128)(2,1)}, bf16[256,128]{1,0:T(8,128)(2,1)S(1)}, u32[]{:S(2)}) %copy-start.3) | copy-done | bytes 65560
  17.0 11.6 %edge_slope.1 = (f32[6144,128]{1,0:T(8,128)}, bf16[6144,256]{1,0:T(8,128)(2,1)}, bf16[6144,128]{1,0:T(8,128)(2,1)}, bf16[2560,128]{1,0:T(8,128)(2,1)}, f32[2048,...) custom-call(s32[48,128]{1,0:T(8,128)} %bitcast.6, ...), custom_call_target="tpu_custom_call" | custom-call | flops 16000000000 | bytes 5000000 | tf_op jit(solution)/shard_map/edge_slope/pallas_call | solution.py:823
  28.6 3.3 %all-to-all-done.arrived_hbm = bf16[16,144,128]{2,1,0:T(8,128)(2,1)} async-done(((bf16[16,144,128]{2,1,0:T(8,128)(2,1)}), bf16[16,144,128]{2,1,0:T(8,128)(2,1)}, u32[]{:S(2)}, u32[]{:S(2)}) %all-to-all-start) | async-done | bytes 589856 | tf_op jit(solution)/shard_map/all_to_all | solution.py:819
  31.9 10.2 %edge_back.1 = (bf16[2048,128]{1,0:T(8,128)(2,1)}, f32[2560,128]{1,0:T(8,128)}, bf16[416,128]{1,0:T(8,128)(2,1)S(1)}, bf16[256,128]{1,0:T(8,128)(2,1)S(1)}, f32[176,128]{1,0:T(8,128)S(1)}) custom-call(s32[48,128]{1,0:T(8,128)} %get-tuple-element.30.stats, bf16[16,144,128]{2,1,0:T(8,128)(2,1)} %all-to-all-done.arrived_hbm, ...), custom_call_target="tpu_custom_call" | custom-call | flops 24000000000 | bytes 8000000 | tf_op jit(solution)/shard_map/edge_back/pallas_call | solution.py:870
  42.2 0.1 collective-permute-start.2
  42.3 1.3 %collective-permute-done.2.first_hbm = bf16[416,128]{1,0:T(8,128)(2,1)S(1)} collective-permute-done((bf16[416,128]{1,0:T(8,128)(2,1)S(1)}, bf16[416,128]{1,0:T(8,128)(2,1)S(1)}, u32[]{:S(2)}, u32[]{:S(2)}) %collective-permute-start.2) | collective-permute-done | bytes 106528 | tf_op jit(solution)/shard_map/ppermute | solution.py:717
  43.6 0.1 add_convert_fusion
  43.7 1.1 %collective-permute-start.3 = (bf16[176,128]{1,0:T(8,128)(2,1)S(1)}, bf16[176,128]{1,0:T(8,128)(2,1)S(1)}, u32[]{:S(2)}, u32[]{:S(2)}) collective-permute-start(bf16[176,128]{1,0:T(8,128)(2,1)S(1)} %add_convert_fusion), channel_id=1, source_target_pairs={{0,2},{1,3},{2,0},{3,1},{4,6},{5,7},{6,4},{7,5},{8,10},{9,11},{10,... | collective-permute-start | bytes 135176 | tf_op jit(solution)/shard_map/ppermute | solution.py:727
  44.7 0.7 %collective-permute-start.7 = (bf16[256,128]{1,0:T(8,128)(2,1)S(1)}, bf16[256,128]{1,0:T(8,128)(2,1)S(1)}, u32[]{:S(2)}, u32[]{:S(2)}) collective-permute-start(bf16[256,128]{1,0:T(8,128)(2,1)S(1)} %get-tuple-element.45), channel_id=1, source_target_pairs={{1,2},{2,1},{3,4},{4,3},{5,6},{6,5},{7,8},{8,7},{9,10},{10,9},{11,... | collective-permute-start | bytes 196616 | tf_op jit(solution)/shard_map/ppermute | solution.py:717
  45.4 2.4 %collective-permute-done.3 = bf16[176,128]{1,0:T(8,128)(2,1)S(1)} collective-permute-done((bf16[176,128]{1,0:T(8,128)(2,1)S(1)}, bf16[176,128]{1,0:T(8,128)(2,1)S(1)}, u32[]{:S(2)}, u32[]{:S(2)}) %collective-permute-start.3) | collective-permute-done | bytes 45088 | tf_op jit(solution)/shard_map/ppermute | solution.py:727
  47.8 1.8 %collective-permute-start.4 = (bf16[192,128]{1,0:T(8,128)(2,1)S(1)}, bf16[192,128]{1,0:T(8,128)(2,1)S(1)}, u32[]{:S(2)}, u32[]{:S(2)}) collective-permute-start(bf16[192,128]{1,0:T(8,128)(2,1)S(1)} %pad_maximum_fusion.1), channel_id=1, source_target_pairs={{0,4},{1,5},{2,6},{3,7},{4,0},{5,1},{6,2},{7,3},{8,12},{9,13},{10,... | collective-permute-start | bytes 147464 | tf_op jit(solution)/shard_map/ppermute | solution.py:727
  49.6 1.8 %collective-permute-start.5 = (bf16[192,128]{1,0:T(8,128)(2,1)S(1)}, bf16[192,128]{1,0:T(8,128)(2,1)S(1)}, u32[]{:S(2)}, u32[]{:S(2)}) collective-permute-start(bf16[192,128]{1,0:T(8,128)(2,1)S(1)} %pad_maximum_fusion.1), channel_id=1, source_target_pairs={{0,8},{1,9},{2,10},{3,11},{4,12},{5,13},{6,14},{7,15},{8,0},{9,1},... | collective-permute-start | bytes 147464 | tf_op jit(solution)/shard_map/ppermute | solution.py:727
  51.3 0.9 %collective-permute-start.6 = (bf16[192,128]{1,0:T(8,128)(2,1)S(1)}, bf16[192,128]{1,0:T(8,128)(2,1)S(1)}, u32[]{:S(2)}, u32[]{:S(2)}) collective-permute-start(bf16[192,128]{1,0:T(8,128)(2,1)S(1)} %pad_maximum_fusion.1), channel_id=1, source_target_pairs={{0,12},{1,13},{2,14},{3,15},{4,8},{5,9},{6,10},{7,11},{8,4},{9,5},... | collective-permute-start | bytes 147464 | tf_op jit(solution)/shard_map/ppermute | solution.py:727
  52.3 0.6 %copy-done.2 = bf16[256,128]{1,0:T(8,128)(2,1)} copy-done((bf16[256,128]{1,0:T(8,128)(2,1)}, bf16[256,128]{1,0:T(8,128)(2,1)S(1)}, u32[]{:S(2)}) %copy-start.2) | copy-done | bytes 65560
  52.9 3.4 %fine_sums.1 = bf16[2048,128]{1,0:T(8,128)(2,1)} custom-call(bf16[2048,128]{1,0:T(8,128)(2,1)} %get-tuple-element.43.grad_hbm, f32[2560,128]{1,0:T(8,128)} %get-tuple-element.44.send_sum_hbm, f32[2048,128]{1,0:T(8,128)} %get-tuple-element.39.slope_sum_hbm, bf16[256,128]{1,0:T(8,128)(2,1)} %weight_hbm.5, bf16[416,128]{1,0:T(8,128)(2,1)} %copy-done, ...), custom_call_target="tpu_custom_call" | custom-call | flops 1000000000 | bytes 4000000 | tf_op jit(solution)/shard_map/fine_sums/pallas_call | solution.py:918
  56.3 1.0 %collective-permute-done.6 = bf16[192,128]{1,0:T(8,128)(2,1)S(1)} collective-permute-done((bf16[192,128]{1,0:T(8,128)(2,1)S(1)}, bf16[192,128]{1,0:T(8,128)(2,1)S(1)}, u32[]{:S(2)}, u32[]{:S(2)}) %collective-permute-start.6) | collective-permute-done | bytes 49184 | tf_op jit(solution)/shard_map/ppermute | solution.py:727
  57.4 0.1 collective-permute-start.8
  57.5 1.4 %collective-permute-done.8.there_ref = f32[288,128]{1,0:T(8,128)S(1)} collective-permute-done((f32[288,128]{1,0:T(8,128)S(1)}, f32[288,128]{1,0:T(8,128)S(1)}, u32[]{:S(2)}, u32[]{:S(2)}) %collective-permute-start.8) | collective-permute-done | bytes 147488 | tf_op jit(solution)/shard_map/ppermute | solution.py:727
  58.9 0.7 %last_terms.1 = (f32[256,128]{1,0:T(8,128)}, f32[128,128]{1,0:T(8,128)}, f32[128,128]{1,0:T(8,128)}, f32[1,128]{1,0:T(1,128)}) custom-call(f32[160,128]{1,0:T(8,128)S(1)} %add_add_fusion.own_ref, bf16[128,128]{1,0:T(8,128)(2,1)S(1)} %get-tuple-element.56.coarse_ref, f32[288,128]{1,0:T(8,128)S(1)} %collective-permute-done.8.there_ref), custom_call_target="tpu_custom_call" | custom-call | tf_op jit(solution)/shard_map/last_terms/pallas_call | solution.py:939
  (24 shorter events, 0.1 us)
Async XLA Ops:
  1.5 14.8 %collective-permute-start = (bf16[256,128]{1,0:T(8,128)(2,1)S(1)}, bf16[256,128]{1,0:T(8,128)(2,1)S(1)}, u32[]{:S(2)}, u32[]{:S(2)}) collective-permute-start(bf16[256,128]{1,0:T(8,128)(2,1)S(1)} %get-tuple-element.58), channel_id=1, source_target_pairs={{0,1},{1,0},{2,3},{3,2},{4,5},{5,4},{6,7},{7,6},{8,9},{9,8},{10,11... | collective-permute-start | bytes 196616 | tf_op jit(solution)/shard_map/ppermute | solution.py:717
  2.0 14.3 %collective-permute-start.1 = (bf16[256,128]{1,0:T(8,128)(2,1)S(1)}, bf16[256,128]{1,0:T(8,128)(2,1)}, u32[]{:S(2)}, u32[]{:S(2)}) collective-permute-start(bf16[256,128]{1,0:T(8,128)(2,1)S(1)} %get-tuple-element.57), channel_id=1, source_target_pairs={{1,2},{2,1},{3,4},{4,3},{5,6},{6,5},{7,8},{8,7},{9,10},{10,9},{11,... | collective-permute-start | bytes 196616 | tf_op jit(solution)/shard_map/ppermute | solution.py:717
  8.1 23.9 %all-to-all-start = ((bf16[16,144,128]{2,1,0:T(8,128)(2,1)}), bf16[16,144,128]{2,1,0:T(8,128)(2,1)}, u32[]{:S(2)}, u32[]{:S(2)}) async-start(bf16[16,144,128]{2,1,0:T(8,128)(2,1)} %get-tuple-element.31), calls=%async_computation | async-start | bytes 1179648 | tf_op jit(solution)/shard_map/all_to_all | solution.py:819
  16.4 0.6 %copy-start.3 = (bf16[256,128]{1,0:T(8,128)(2,1)}, bf16[256,128]{1,0:T(8,128)(2,1)S(1)}, u32[]{:S(2)}) copy-start(bf16[256,128]{1,0:T(8,128)(2,1)S(1)} %collective-permute-done.first_hbm) | copy-start | bytes 196612
  31.9 11.6 %copy-start.1 = (pred[176]{0:T(512)(128)(4,1)S(1)}, pred[176]{0:T(512)(128)(4,1)}, u32[]{:S(2)}) copy-start(pred[176]{0:T(512)(128)(4,1)} %constant.14.clone.1) | copy-start | bytes 532
  42.2 1.4 %collective-permute-start.2 = (bf16[416,128]{1,0:T(8,128)(2,1)S(1)}, bf16[416,128]{1,0:T(8,128)(2,1)S(1)}, u32[]{:S(2)}, u32[]{:S(2)}) collective-permute-start(bf16[416,128]{1,0:T(8,128)(2,1)S(1)} %get-tuple-element.42), channel_id=1, source_target_pairs={{0,1},{1,0},{2,3},{3,2},{4,5},{5,4},{6,7},{7,6},{8,9},{9,8},{10,11... | collective-permute-start | bytes 319496 | tf_op jit(solution)/shard_map/ppermute | solution.py:717
  43.6 8.7 %copy-start = (bf16[416,128]{1,0:T(8,128)(2,1)}, bf16[416,128]{1,0:T(8,128)(2,1)S(1)}, u32[]{:S(2)}) copy-start(bf16[416,128]{1,0:T(8,128)(2,1)S(1)} %collective-permute-done.2.first_hbm) | copy-start | bytes 319492
  43.7 4.1 %collective-permute-start.3 = (bf16[176,128]{1,0:T(8,128)(2,1)S(1)}, bf16[176,128]{1,0:T(8,128)(2,1)S(1)}, u32[]{:S(2)}, u32[]{:S(2)}) collective-permute-start(bf16[176,128]{1,0:T(8,128)(2,1)S(1)} %add_convert_fusion), channel_id=1, source_target_pairs={{0,2},{1,3},{2,0},{3,1},{4,6},{5,7},{6,4},{7,5},{8,10},{9,11},{10,... | collective-permute-start | bytes 135176 | tf_op jit(solution)/shard_map/ppermute | solution.py:727
  44.7 7.6 %collective-permute-start.7 = (bf16[256,128]{1,0:T(8,128)(2,1)S(1)}, bf16[256,128]{1,0:T(8,128)(2,1)S(1)}, u32[]{:S(2)}, u32[]{:S(2)}) collective-permute-start(bf16[256,128]{1,0:T(8,128)(2,1)S(1)} %get-tuple-element.45), channel_id=1, source_target_pairs={{1,2},{2,1},{3,4},{4,3},{5,6},{6,5},{7,8},{8,7},{9,10},{10,9},{11,... | collective-permute-start | bytes 196616 | tf_op jit(solution)/shard_map/ppermute | solution.py:717
  47.8 8.4 %collective-permute-start.4 = (bf16[192,128]{1,0:T(8,128)(2,1)S(1)}, bf16[192,128]{1,0:T(8,128)(2,1)S(1)}, u32[]{:S(2)}, u32[]{:S(2)}) collective-permute-start(bf16[192,128]{1,0:T(8,128)(2,1)S(1)} %pad_maximum_fusion.1), channel_id=1, source_target_pairs={{0,4},{1,5},{2,6},{3,7},{4,0},{5,1},{6,2},{7,3},{8,12},{9,13},{10,... | collective-permute-start | bytes 147464 | tf_op jit(solution)/shard_map/ppermute | solution.py:727
  49.6 6.7 %collective-permute-start.5 = (bf16[192,128]{1,0:T(8,128)(2,1)S(1)}, bf16[192,128]{1,0:T(8,128)(2,1)S(1)}, u32[]{:S(2)}, u32[]{:S(2)}) collective-permute-start(bf16[192,128]{1,0:T(8,128)(2,1)S(1)} %pad_maximum_fusion.1), channel_id=1, source_target_pairs={{0,8},{1,9},{2,10},{3,11},{4,12},{5,13},{6,14},{7,15},{8,0},{9,1},... | collective-permute-start | bytes 147464 | tf_op jit(solution)/shard_map/ppermute | solution.py:727
  51.3 6.0 %collective-permute-start.6 = (bf16[192,128]{1,0:T(8,128)(2,1)S(1)}, bf16[192,128]{1,0:T(8,128)(2,1)S(1)}, u32[]{:S(2)}, u32[]{:S(2)}) collective-permute-start(bf16[192,128]{1,0:T(8,128)(2,1)S(1)} %pad_maximum_fusion.1), channel_id=1, source_target_pairs={{0,12},{1,13},{2,14},{3,15},{4,8},{5,9},{6,10},{7,11},{8,4},{9,5},... | collective-permute-start | bytes 147464 | tf_op jit(solution)/shard_map/ppermute | solution.py:727
  52.3 0.6 %copy-start.2 = (bf16[256,128]{1,0:T(8,128)(2,1)}, bf16[256,128]{1,0:T(8,128)(2,1)S(1)}, u32[]{:S(2)}) copy-start(bf16[256,128]{1,0:T(8,128)(2,1)S(1)} %collective-permute-done.7.second_hbm) | copy-start | bytes 196612
  57.4 1.4 %collective-permute-start.8 = (f32[288,128]{1,0:T(8,128)S(1)}, f32[288,128]{1,0:T(8,128)S(1)}, u32[]{:S(2)}, u32[]{:S(2)}) collective-permute-start(f32[288,128]{1,0:T(8,128)S(1)} %pad_maximum_fusion), channel_id=1, source_target_pairs={{0,1},{1,0},{2,3},{3,2},{4,5},{5,4},{6,7},{7,6},{8,9},{9,8},{10,11... | collective-permute-start | bytes 442376 | tf_op jit(solution)/shard_map/ppermute | solution.py:727

commit v3 on v2

--- a/solution.py
+++ b/solution.py
@@ -639,14 +639,16 @@
     weight_hbm,
     first_hbm,
     second_hbm,
-    fine_ref,
+    fine_hbm,
     grad_table,
     send_sum,
     slope_sum,
     weight_ref,
     first_ref,
     second_ref,
+    fine_ref,
     arrivals,
+    leaving,
 ):
     fine_count = fine_ref.shape[0]
     for copy in fetch(
@@ -659,20 +661,29 @@
     half = first_ref.shape[0] - HB
     one, two = first_ref[half:, :].astype(F32), second_ref[...].astype(F32)
     from_next, from_prev = jnp.where(odd == 0, one, two), jnp.where(odd == 0, two, one)
+    send_weight, recv_weight = weight_ref[0:LANES, :], weight_ref[LANES:, :]
+    weights = jnp.concatenate([send_weight, send_weight, recv_weight, recv_weight], axis=1)
+    copies = []
     for first in range(0, fine_count, SPAN):
         at = slice(first, first + SPAN)
         moved = slice(HB + first, HB + first + SPAN)
         grad = grad_table[at, :].astype(F32)
-        summed = (
-            grad
-            + back(send_sum[moved, :], weight_ref[0:LANES, :])
-            + back(grad * slope_sum[at, :], weight_ref[LANES:, :])
-        )
+        parts = two_parts(send_sum[moved, :]) + two_parts(grad * slope_sum[at, :])
+        summed = grad + dot(jnp.concatenate(parts, axis=1), weights, NT)
         if first == 0:
             summed += from_prev
         if first == fine_count - SPAN:
             summed += from_next
         fine_ref[at, :] = summed.astype(BF16)
+        rows = pl.ds(first, SPAN)
+        copies.append(
+            pltpu.make_async_copy(
+                fine_ref.at[rows], fine_hbm.at[rows], leaving.at[first // SPAN]
+            )
+        )
+        copies[-1].start()
+    for copy in copies:
+        copy.wait()
 
 
 def last_kernel(
@@ -774,6 +785,7 @@
     payload = capacity + EXTRA
     edge_rows = edge_count // LANES
     window_count = fine_count + 2 * HB
+    fine_blocks = fine_count // SPAN
     params = pltpu.CompilerParams(vmem_limit_bytes=64 * 1024 * 1024 - 256 * 1024)
     roomy = pltpu.CompilerParams(vmem_limit_bytes=62 * 1024 * 1024)
     anywhere = pl.BlockSpec(memory_space=pl.ANY)
@@ -919,6 +931,7 @@
         fine_kernel,
         out_shape=jax.ShapeDtypeStruct((fine_count, LANES), BF16),
         in_specs=[anywhere] * 6,
+        out_specs=anywhere,
         scratch_shapes=[
             pltpu.VMEM((fine_count, LANES), BF16),
             pltpu.VMEM((window_count, LANES), F32),
@@ -926,7 +939,9 @@
             pltpu.VMEM((2 * LANES, LANES), BF16),
             pltpu.VMEM((half + HB, LANES), BF16),
             pltpu.VMEM((HB, LANES), BF16),
+            pltpu.VMEM((fine_count, LANES), BF16),
             pltpu.SemaphoreType.DMA((6,)),
+            pltpu.SemaphoreType.DMA((fine_blocks,)),
         ],
         compiler_params=pltpu.CompilerParams(vmem_limit_bytes=64 * 1024 * 1024 - 1536 * 1024),
         cost_estimate=pl.CostEstimate(

time: 60 us -> 60.1 us (level)
  transfers between devices with their start and end apart: 10 -> 10, of which waited for: 5 -> 6; matrix products, arithmetic and copies ran while one was open for 0% -> 0% of each run, Pallas kernels for 33% -> 33%
where the time goes in v3:
time: 60.1 us; the launch traced here: 59.6 us
  Pallas kernels  30.6 us (51%)
  starting transfers between devices  16.4 us (27%)
  waiting for transfers between devices  9.46 us (16%)
  local copies, waits for them, and re-layouts  1.26 us (2%)
  other arithmetic  1.08 us (2%)
  between operations  0.81 us (1%)
    pallas_call x1, Pallas kernels, per_device(): pl.pallas_call(slope_kernel, out_shape=(jax.ShapeDtypeStruct((edge_count,...  11.6 us
    pallas_call x1, Pallas kernels, per_device(): pl.pallas_call(edge_kernel, out_shape=(jax.ShapeDtypeStruct((fine_count,...  10.2 us
    all_to_all x1, starting transfers between devices, per_device(): lax.all_to_all(sent, 'curve', split_axis=0, concat_axis=0, tiled=True)  8.27 us
    ppermute x5, starting transfers between devices, swapped(): return lax.ppermute(values, 'curve', [(i, i ^ hops) for i in range(peers)])  5.61 us
    ppermute x5, waiting for transfers between devices, swapped(): return lax.ppermute(values, 'curve', [(i, i ^ hops) for i in range(peers)])  4.85 us
    pallas_call x1, Pallas kernels, per_device(): pl.pallas_call(functools.partial(coarse_kernel, peers), out_shape=(jax.Sh...  4.74 us
    all_to_all x1, waiting for transfers between devices, per_device(): lax.all_to_all(sent, 'curve', split_axis=0, concat_axis=0, tiled=True)  3.33 us
    pallas_call x1, Pallas kernels, per_device(): pl.pallas_call(fine_kernel, out_shape=jax.ShapeDtypeStruct((fine_count, L...  3.26 us
  transfers between devices with their start and end apart: 10, of which 6 were waited for; matrix products, arithmetic and copies ran while one was open for 0% of the time, Pallas kernels for 33%

profile of v3, /device:TPU:0, one launch (start us, length us, event | category | flops | bytes accessed | tf_op | source)
XLA Modules:
  0.0 59.6 jit_solution(16149222709702623170)
XLA Ops:
  0.6 0.9 %broadcast_select_fusion = (bf16[256,128]{1,0:T(8,128)(2,1)S(1)}, bf16[256,128]{1,0:T(8,128)(2,1)S(1)}) fusion(pred[]{:T(512)S(6)} %eq.3, bf16[2048,128]{1,0:T(8,128)(2,1)} %fine_hbm.1), kind=kLoop, calls=%fused_computation.4 | loop fusion | flops 65536 | bytes 262145 | tf_op jit(solution)/shard_map/jit(_where)/select_n | solution.py:796
  1.5 0.5 collective-permute-start
  2.0 1.3 %collective-permute-start.1 = (bf16[256,128]{1,0:T(8,128)(2,1)S(1)}, bf16[256,128]{1,0:T(8,128)(2,1)}, u32[]{:S(2)}, u32[]{:S(2)}) collective-permute-start(bf16[256,128]{1,0:T(8,128)(2,1)S(1)} %get-tuple-element.57), channel_id=1, source_target_pairs={{1,2},{2,1},{3,4},{4,3},{5,6},{6,5},{7,8},{8,7},{9,10},{10,9},{11,... | collective-permute-start | bytes 196616 | tf_op jit(solution)/shard_map/ppermute | solution.py:728
  3.3 4.7 %coarse_block.1 = (bf16[16,144,128]{2,1,0:T(8,128)(2,1)}, f32[64,128]{1,0:T(8,128)}) custom-call(bf16[1024,128]{1,0:T(8,128)(2,1)} %latent_ref.1, bf16[1024,128]{1,0:T(8,128)(2,1)} %grad_ref.1, bf16[2,1024]{1,0:T(2,128)(2,1)} %weights_ref.1, s32[16,128]{1,0:T(8,128)} %bitcast.8, bf16[128,128]{1,0:T(8,128)(2,1)} %w_in_ref.1, bf16[128,128]{1,0:T(8,128)(2,1)} %w_out_ref.1, ...), custom_call_target="tpu_custom_call" | custom-call | flops 2000000000 | bytes 2000000 | tf_op jit(solution)/shard_map/coarse_block/pallas_call | solution.py:798
  8.1 8.3 %all-to-all-start = ((bf16[16,144,128]{2,1,0:T(8,128)(2,1)}), bf16[16,144,128]{2,1,0:T(8,128)(2,1)}, u32[]{:S(2)}, u32[]{:S(2)}) async-start(bf16[16,144,128]{2,1,0:T(8,128)(2,1)} %get-tuple-element.31), calls=%async_computation | async-start | bytes 1179648 | tf_op jit(solution)/shard_map/all_to_all | solution.py:831
  16.4 0.6 %copy-done.3 = bf16[256,128]{1,0:T(8,128)(2,1)} copy-done((bf16[256,128]{1,0:T(8,128)(2,1)}, bf16[256,128]{1,0:T(8,128)(2,1)S(1)}, u32[]{:S(2)}) %copy-start.3) | copy-done | bytes 65560
  17.0 11.6 %edge_slope.1 = (f32[6144,128]{1,0:T(8,128)}, bf16[6144,256]{1,0:T(8,128)(2,1)}, bf16[6144,128]{1,0:T(8,128)(2,1)}, bf16[2560,128]{1,0:T(8,128)(2,1)}, f32[2048,...) custom-call(s32[48,128]{1,0:T(8,128)} %bitcast.6, ...), custom_call_target="tpu_custom_call" | custom-call | flops 16000000000 | bytes 5000000 | tf_op jit(solution)/shard_map/edge_slope/pallas_call | solution.py:835
  28.6 3.3 %all-to-all-done.arrived_hbm = bf16[16,144,128]{2,1,0:T(8,128)(2,1)} async-done(((bf16[16,144,128]{2,1,0:T(8,128)(2,1)}), bf16[16,144,128]{2,1,0:T(8,128)(2,1)}, u32[]{:S(2)}, u32[]{:S(2)}) %all-to-all-start) | async-done | bytes 589856 | tf_op jit(solution)/shard_map/all_to_all | solution.py:831
  31.9 10.2 %edge_back.1 = (bf16[2048,128]{1,0:T(8,128)(2,1)}, f32[2560,128]{1,0:T(8,128)}, bf16[416,128]{1,0:T(8,128)(2,1)S(1)}, bf16[256,128]{1,0:T(8,128)(2,1)S(1)}, f32[176,128]{1,0:T(8,128)S(1)}) custom-call(s32[48,128]{1,0:T(8,128)} %get-tuple-element.30.stats, bf16[16,144,128]{2,1,0:T(8,128)(2,1)} %all-to-all-done.arrived_hbm, ...), custom_call_target="tpu_custom_call" | custom-call | flops 24000000000 | bytes 8000000 | tf_op jit(solution)/shard_map/edge_back/pallas_call | solution.py:882
  42.2 0.1 collective-permute-start.2
  42.3 1.3 %collective-permute-done.2.first_hbm = bf16[416,128]{1,0:T(8,128)(2,1)S(1)} collective-permute-done((bf16[416,128]{1,0:T(8,128)(2,1)S(1)}, bf16[416,128]{1,0:T(8,128)(2,1)S(1)}, u32[]{:S(2)}, u32[]{:S(2)}) %collective-permute-start.2) | collective-permute-done | bytes 106528 | tf_op jit(solution)/shard_map/ppermute | solution.py:728
  43.6 0.1 add_convert_fusion
  43.7 1.1 %collective-permute-start.3 = (bf16[176,128]{1,0:T(8,128)(2,1)S(1)}, bf16[176,128]{1,0:T(8,128)(2,1)S(1)}, u32[]{:S(2)}, u32[]{:S(2)}) collective-permute-start(bf16[176,128]{1,0:T(8,128)(2,1)S(1)} %add_convert_fusion), channel_id=1, source_target_pairs={{0,2},{1,3},{2,0},{3,1},{4,6},{5,7},{6,4},{7,5},{8,10},{9,11},{10,... | collective-permute-start | bytes 135176 | tf_op jit(solution)/shard_map/ppermute | solution.py:738
  44.8 0.7 %collective-permute-start.7 = (bf16[256,128]{1,0:T(8,128)(2,1)S(1)}, bf16[256,128]{1,0:T(8,128)(2,1)S(1)}, u32[]{:S(2)}, u32[]{:S(2)}) collective-permute-start(bf16[256,128]{1,0:T(8,128)(2,1)S(1)} %get-tuple-element.45), channel_id=1, source_target_pairs={{1,2},{2,1},{3,4},{4,3},{5,6},{6,5},{7,8},{8,7},{9,10},{10,9},{11,... | collective-permute-start | bytes 196616 | tf_op jit(solution)/shard_map/ppermute | solution.py:728
  45.4 2.4 %collective-permute-done.3 = bf16[176,128]{1,0:T(8,128)(2,1)S(1)} collective-permute-done((bf16[176,128]{1,0:T(8,128)(2,1)S(1)}, bf16[176,128]{1,0:T(8,128)(2,1)S(1)}, u32[]{:S(2)}, u32[]{:S(2)}) %collective-permute-start.3) | collective-permute-done | bytes 45088 | tf_op jit(solution)/shard_map/ppermute | solution.py:738
  47.8 1.8 %collective-permute-start.4 = (bf16[192,128]{1,0:T(8,128)(2,1)S(1)}, bf16[192,128]{1,0:T(8,128)(2,1)S(1)}, u32[]{:S(2)}, u32[]{:S(2)}) collective-permute-start(bf16[192,128]{1,0:T(8,128)(2,1)S(1)} %pad_maximum_fusion.1), channel_id=1, source_target_pairs={{0,4},{1,5},{2,6},{3,7},{4,0},{5,1},{6,2},{7,3},{8,12},{9,13},{10,... | collective-permute-start | bytes 147464 | tf_op jit(solution)/shard_map/ppermute | solution.py:738
  49.6 1.7 %collective-permute-start.5 = (bf16[192,128]{1,0:T(8,128)(2,1)S(1)}, bf16[192,128]{1,0:T(8,128)(2,1)S(1)}, u32[]{:S(2)}, u32[]{:S(2)}) collective-permute-start(bf16[192,128]{1,0:T(8,128)(2,1)S(1)} %pad_maximum_fusion.1), channel_id=1, source_target_pairs={{0,8},{1,9},{2,10},{3,11},{4,12},{5,13},{6,14},{7,15},{8,0},{9,1},... | collective-permute-start | bytes 147464 | tf_op jit(solution)/shard_map/ppermute | solution.py:738
  51.4 0.9 %collective-permute-start.6 = (bf16[192,128]{1,0:T(8,128)(2,1)S(1)}, bf16[192,128]{1,0:T(8,128)(2,1)S(1)}, u32[]{:S(2)}, u32[]{:S(2)}) collective-permute-start(bf16[192,128]{1,0:T(8,128)(2,1)S(1)} %pad_maximum_fusion.1), channel_id=1, source_target_pairs={{0,12},{1,13},{2,14},{3,15},{4,8},{5,9},{6,10},{7,11},{8,4},{9,5},... | collective-permute-start | bytes 147464 | tf_op jit(solution)/shard_map/ppermute | solution.py:738
  52.3 0.6 %copy-done.2 = bf16[256,128]{1,0:T(8,128)(2,1)} copy-done((bf16[256,128]{1,0:T(8,128)(2,1)}, bf16[256,128]{1,0:T(8,128)(2,1)S(1)}, u32[]{:S(2)}) %copy-start.2) | copy-done | bytes 65560
  52.9 3.3 %fine_sums.1 = bf16[2048,128]{1,0:T(8,128)(2,1)} custom-call(bf16[2048,128]{1,0:T(8,128)(2,1)} %get-tuple-element.43.grad_hbm, f32[2560,128]{1,0:T(8,128)} %get-tuple-element.44.send_sum_hbm, f32[2048,128]{1,0:T(8,128)} %get-tuple-element.39.slope_sum_hbm, bf16[256,128]{1,0:T(8,128)(2,1)} %weight_hbm.5, bf16[416,128]{1,0:T(8,128)(2,1)} %copy-done, ...), custom_call_target="tpu_custom_call" | custom-call | flops 1000000000 | bytes 4000000 | tf_op jit(solution)/shard_map/fine_sums/pallas_call | solution.py:930
  56.2 0.1 collective-permute-done.5
  56.3 1.1 %collective-permute-done.6 = bf16[192,128]{1,0:T(8,128)(2,1)S(1)} collective-permute-done((bf16[192,128]{1,0:T(8,128)(2,1)S(1)}, bf16[192,128]{1,0:T(8,128)(2,1)S(1)}, u32[]{:S(2)}, u32[]{:S(2)}) %collective-permute-start.6) | collective-permute-done | bytes 49184 | tf_op jit(solution)/shard_map/ppermute | solution.py:738
  57.5 1.4 %collective-permute-done.8.there_ref = f32[288,128]{1,0:T(8,128)S(1)} collective-permute-done((f32[288,128]{1,0:T(8,128)S(1)}, f32[288,128]{1,0:T(8,128)S(1)}, u32[]{:S(2)}, u32[]{:S(2)}) %collective-permute-start.8) | collective-permute-done | bytes 147488 | tf_op jit(solution)/shard_map/ppermute | solution.py:738
  58.9 0.7 %last_terms.1 = (f32[256,128]{1,0:T(8,128)}, f32[128,128]{1,0:T(8,128)}, f32[128,128]{1,0:T(8,128)}, f32[1,128]{1,0:T(1,128)}) custom-call(f32[160,128]{1,0:T(8,128)S(1)} %add_add_fusion.own_ref, bf16[128,128]{1,0:T(8,128)(2,1)S(1)} %get-tuple-element.56.coarse_ref, f32[288,128]{1,0:T(8,128)S(1)} %collective-permute-done.8.there_ref), custom_call_target="tpu_custom_call" | custom-call | tf_op jit(solution)/shard_map/last_terms/pallas_call | solution.py:954
  (24 shorter events, 0.2 us)
Async XLA Ops:
  1.5 14.8 %collective-permute-start = (bf16[256,128]{1,0:T(8,128)(2,1)S(1)}, bf16[256,128]{1,0:T(8,128)(2,1)S(1)}, u32[]{:S(2)}, u32[]{:S(2)}) collective-permute-start(bf16[256,128]{1,0:T(8,128)(2,1)S(1)} %get-tuple-element.58), channel_id=1, source_target_pairs={{0,1},{1,0},{2,3},{3,2},{4,5},{5,4},{6,7},{7,6},{8,9},{9,8},{10,11... | collective-permute-start | bytes 196616 | tf_op jit(solution)/shard_map/ppermute | solution.py:728
  2.0 14.3 %collective-permute-start.1 = (bf16[256,128]{1,0:T(8,128)(2,1)S(1)}, bf16[256,128]{1,0:T(8,128)(2,1)}, u32[]{:S(2)}, u32[]{:S(2)}) collective-permute-start(bf16[256,128]{1,0:T(8,128)(2,1)S(1)} %get-tuple-element.57), channel_id=1, source_target_pairs={{1,2},{2,1},{3,4},{4,3},{5,6},{6,5},{7,8},{8,7},{9,10},{10,9},{11,... | collective-permute-start | bytes 196616 | tf_op jit(solution)/shard_map/ppermute | solution.py:728
  8.1 23.9 %all-to-all-start = ((bf16[16,144,128]{2,1,0:T(8,128)(2,1)}), bf16[16,144,128]{2,1,0:T(8,128)(2,1)}, u32[]{:S(2)}, u32[]{:S(2)}) async-start(bf16[16,144,128]{2,1,0:T(8,128)(2,1)} %get-tuple-element.31), calls=%async_computation | async-start | bytes 1179648 | tf_op jit(solution)/shard_map/all_to_all | solution.py:831
  16.4 0.6 %copy-start.3 = (bf16[256,128]{1,0:T(8,128)(2,1)}, bf16[256,128]{1,0:T(8,128)(2,1)S(1)}, u32[]{:S(2)}) copy-start(bf16[256,128]{1,0:T(8,128)(2,1)S(1)} %collective-permute-done.first_hbm) | copy-start | bytes 196612
  31.9 11.6 %copy-start.1 = (pred[176]{0:T(512)(128)(4,1)S(1)}, pred[176]{0:T(512)(128)(4,1)}, u32[]{:S(2)}) copy-start(pred[176]{0:T(512)(128)(4,1)} %constant.14.clone.1) | copy-start | bytes 532
  42.2 1.4 %collective-permute-start.2 = (bf16[416,128]{1,0:T(8,128)(2,1)S(1)}, bf16[416,128]{1,0:T(8,128)(2,1)S(1)}, u32[]{:S(2)}, u32[]{:S(2)}) collective-permute-start(bf16[416,128]{1,0:T(8,128)(2,1)S(1)} %get-tuple-element.42), channel_id=1, source_target_pairs={{0,1},{1,0},{2,3},{3,2},{4,5},{5,4},{6,7},{7,6},{8,9},{9,8},{10,11... | collective-permute-start | bytes 319496 | tf_op jit(solution)/shard_map/ppermute | solution.py:728
  43.6 8.7 %copy-start = (bf16[416,128]{1,0:T(8,128)(2,1)}, bf16[416,128]{1,0:T(8,128)(2,1)S(1)}, u32[]{:S(2)}) copy-start(bf16[416,128]{1,0:T(8,128)(2,1)S(1)} %collective-permute-done.2.first_hbm) | copy-start | bytes 319492
  43.7 4.1 %collective-permute-start.3 = (bf16[176,128]{1,0:T(8,128)(2,1)S(1)}, bf16[176,128]{1,0:T(8,128)(2,1)S(1)}, u32[]{:S(2)}, u32[]{:S(2)}) collective-permute-start(bf16[176,128]{1,0:T(8,128)(2,1)S(1)} %add_convert_fusion), channel_id=1, source_target_pairs={{0,2},{1,3},{2,0},{3,1},{4,6},{5,7},{6,4},{7,5},{8,10},{9,11},{10,... | collective-permute-start | bytes 135176 | tf_op jit(solution)/shard_map/ppermute | solution.py:738
  44.8 7.5 %collective-permute-start.7 = (bf16[256,128]{1,0:T(8,128)(2,1)S(1)}, bf16[256,128]{1,0:T(8,128)(2,1)S(1)}, u32[]{:S(2)}, u32[]{:S(2)}) collective-permute-start(bf16[256,128]{1,0:T(8,128)(2,1)S(1)} %get-tuple-element.45), channel_id=1, source_target_pairs={{1,2},{2,1},{3,4},{4,3},{5,6},{6,5},{7,8},{8,7},{9,10},{10,9},{11,... | collective-permute-start | bytes 196616 | tf_op jit(solution)/shard_map/ppermute | solution.py:728
  47.8 8.4 %collective-permute-start.4 = (bf16[192,128]{1,0:T(8,128)(2,1)S(1)}, bf16[192,128]{1,0:T(8,128)(2,1)S(1)}, u32[]{:S(2)}, u32[]{:S(2)}) collective-permute-start(bf16[192,128]{1,0:T(8,128)(2,1)S(1)} %pad_maximum_fusion.1), channel_id=1, source_target_pairs={{0,4},{1,5},{2,6},{3,7},{4,0},{5,1},{6,2},{7,3},{8,12},{9,13},{10,... | collective-permute-start | bytes 147464 | tf_op jit(solution)/shard_map/ppermute | solution.py:738
  49.6 6.7 %collective-permute-start.5 = (bf16[192,128]{1,0:T(8,128)(2,1)S(1)}, bf16[192,128]{1,0:T(8,128)(2,1)S(1)}, u32[]{:S(2)}, u32[]{:S(2)}) collective-permute-start(bf16[192,128]{1,0:T(8,128)(2,1)S(1)} %pad_maximum_fusion.1), channel_id=1, source_target_pairs={{0,8},{1,9},{2,10},{3,11},{4,12},{5,13},{6,14},{7,15},{8,0},{9,1},... | collective-permute-start | bytes 147464 | tf_op jit(solution)/shard_map/ppermute | solution.py:738
  51.4 6.0 %collective-permute-start.6 = (bf16[192,128]{1,0:T(8,128)(2,1)S(1)}, bf16[192,128]{1,0:T(8,128)(2,1)S(1)}, u32[]{:S(2)}, u32[]{:S(2)}) collective-permute-start(bf16[192,128]{1,0:T(8,128)(2,1)S(1)} %pad_maximum_fusion.1), channel_id=1, source_target_pairs={{0,12},{1,13},{2,14},{3,15},{4,8},{5,9},{6,10},{7,11},{8,4},{9,5},... | collective-permute-start | bytes 147464 | tf_op jit(solution)/shard_map/ppermute | solution.py:738
  52.3 0.6 %copy-start.2 = (bf16[256,128]{1,0:T(8,128)(2,1)}, bf16[256,128]{1,0:T(8,128)(2,1)S(1)}, u32[]{:S(2)}) copy-start(bf16[256,128]{1,0:T(8,128)(2,1)S(1)} %collective-permute-done.7.second_hbm) | copy-start | bytes 196612
  57.4 1.4 %collective-permute-start.8 = (f32[288,128]{1,0:T(8,128)S(1)}, f32[288,128]{1,0:T(8,128)S(1)}, u32[]{:S(2)}, u32[]{:S(2)}) collective-permute-start(f32[288,128]{1,0:T(8,128)S(1)} %pad_maximum_fusion), channel_id=1, source_target_pairs={{0,1},{1,0},{2,3},{3,2},{4,5},{5,4},{6,7},{7,6},{8,9},{9,8},{10,11... | collective-permute-start | bytes 442376 | tf_op jit(solution)/shard_map/ppermute | solution.py:738
